TPU v7x, 256 devices: a whole 4x4x8 slice. The times are simulated.
256 devices in a mesh: dom: 32 (over y, x, core), blk: 8 (over z).
Axes of the slice: x: 4, y: 4, z: 8, core: 2. Of those that a mesh axis runs over, the one named last changes fastest.
Arguments:
- source: bfloat16 [4096, 192], P(('dom', 'blk')), may hold values from -6 to 6
- lam_init: bfloat16 [4096, 192], P(('dom', 'blk')), may hold values from -6 to 6
- offd: bfloat16 [4096, 192, 1152], P(('dom', 'blk')), may hold values from -0.1875 to 0.1875
- dinv: bfloat16 [192, 786432], P(None, ('dom', 'blk')), may hold values from -0.4375 to 0.4375
- colidx: int32 [4096, 6], P(('dom', 'blk')), may hold values from 0 to 191
- face_list: int32 [32, 64], P('dom'), may hold values from 0 to 127
- partner: int32 [32], P('dom'), may hold values from 0 to 31, as said below
- perf_block: int32 [32768], P(('dom', 'blk')), may hold values from 0 to 15
- perf_well: int32 [32768], P(('dom', 'blk')), may hold values from 0 to 63
- perf_sens: bfloat16 [32768, 192], P(('dom', 'blk')), may hold values from -0.21875 to 0.21875
- obj_weight: float32 [1024], replicated, may hold values from 0.5 to 2
- step_index: int32 [1], replicated, may hold values from 0 to 1023
Outputs:
- adjoint: float32 [4096, 192], P(('dom', 'blk'))
- control_grad: float32 [2048], P(('dom', 'blk'))
Inputs may be any that keep to these rules, and one draw needn't show every extreme that they name: Below 128 an own block of the partition, from 128 on halo block colidx - 128. `face_list`: blocks of the partition's own 128, repeats possible. A pairing: partner[p] != p and partner[partner[p]] == p.
All inputs are finite; a program needn't handle non-finite values.
Results may differ from a plain program's by a relative error of at most 0.0054.
Values may be sent and summed in bfloat16 or wider, within the bound.
No kernel may reach another device: no remote copies, remote signals or barrier semaphores. Data moves between devices by JAX's collectives and lax.ppermute only.
A program may use at most 64 MiB of HBM per device.

v0:
```python
import jax
import jax.numpy as jnp
from jax import lax
from jax.sharding import PartitionSpec as P

WP = 64


def cross_partition(face_rows, partner_id):
    slot_count = lax.axis_size("dom")
    onehot = (jnp.arange(slot_count, dtype=jnp.int32) == partner_id).astype(jnp.bfloat16)
    outgoing = onehot[:, None, None] * face_rows[None, :, :]
    incoming = lax.all_to_all(outgoing, "dom", split_axis=0, concat_axis=0, tiled=True)
    halo_blocks = lax.dynamic_index_in_dim(incoming, partner_id, 0, keepdims=False)
    return halo_blocks


def extended_state(state, face_index, partner_id):
    partition = lax.all_gather(state, "blk", axis=0, tiled=True)
    halo_blocks = cross_partition(partition[face_index], partner_id)
    return jnp.concatenate([partition, halo_blocks], axis=0)


def sweep_once(state, forcing, offd, inverses, colidx, face_index, partner_id):
    extended = extended_state(state, face_index, partner_id)
    picked = extended[colidx].reshape(colidx.shape[0], -1)
    coupled = jnp.einsum("bim,bm->bi", offd, picked, preferred_element_type=jnp.float32)
    residual_rhs = (forcing - coupled).astype(jnp.bfloat16)
    return jnp.einsum("ibj,bj->bi", inverses, residual_rhs, preferred_element_type=jnp.float32)


def body(
    source,
    lam_init,
    offd,
    dinv,
    colidx,
    face_list,
    partner,
    perf_block,
    perf_well,
    perf_sens,
    obj_weight,
    step_index,
):
    weight = lax.dynamic_index_in_dim(obj_weight, step_index[0], 0, keepdims=False)
    forcing = weight * source.astype(jnp.float32)
    width = source.shape[1]
    inverses = dinv.reshape(width, source.shape[0], width)
    face_index = face_list[0]
    partner_id = partner[0]
    first_pass = sweep_once(
        lam_init, forcing, offd, inverses, colidx, face_index, partner_id
    ).astype(jnp.bfloat16)
    adjoint = sweep_once(first_pass, forcing, offd, inverses, colidx, face_index, partner_id)
    contrib = jnp.sum(perf_sens.astype(jnp.float32) * adjoint[perf_block], axis=1)
    onehot = (perf_well[:, None] == jnp.arange(WP, dtype=jnp.int32)[None, :]).astype(jnp.float32)
    well_terms = -jnp.dot(contrib, onehot, precision=lax.Precision.HIGHEST)
    control_grad = lax.psum_scatter(well_terms, "blk", scatter_dimension=0, tiled=True)
    return (adjoint, control_grad)


def solution(mesh):
    placed = (
        P(("dom", "blk"), None),
        P(("dom", "blk"), None),
        P(("dom", "blk"), None, None),
        P(None, ("dom", "blk")),
        P(("dom", "blk"), None),
        P("dom", None),
        P("dom"),
        P(("dom", "blk")),
        P(("dom", "blk")),
        P(("dom", "blk"), None),
        P(),
        P(),
    )
    return jax.shard_map(
        body,
        mesh=mesh,
        in_specs=placed,
        out_specs=(P(("dom", "blk"), None), P(("dom", "blk"))),
        check_vma=False,
    )
```

profile of v0, /device:TPU:2, one launch (start us, length us, event | category | flops | bytes accessed | tf_op | source)
XLA Modules:
  0.0 136.8 jit_solution(17076358415785166185)
XLA Ops:
  1.3 28.4 %all_gather.6 = bf16[128,192]{1,0:T(8,128)(2,1)S(1)} all-gather(bf16[16,192]{1,0:T(8,128)(2,1)} %param.13), channel_id=1, replica_groups=mesh['dom'=32,'blk'=8] {'blk'}, dimensions={0}, use_global_device_ids=true | all-gather | bytes 55296 | tf_op jit(solution)/shard_map/all_gather | solution.py:19
  29.7 0.7 fusion.10
  30.3 0.7 gather_fusion
  31.1 1.2 broadcast_multiply_fusion.1
  32.2 7.7 %all-to-all-start = ((bf16[32,64,192]{2,1,0:T(8,128)(2,1)}), bf16[32,64,192]{2,1,0:T(8,128)(2,1)}, u32[]{:S(2)}, u32[]{:S(2)}) async-start(bf16[32,64,192]{2,1,0:T(8,128)(2,1)} %broadcast_multiply_fusion.1), calls=%async_computation | async-start | bytes 2097152 | tf_op jit(solution)/shard_map/all_to_all | solution.py:13
  40.8 0.7 copy.29
  41.5 1.3 dynamic_slice.11
  42.8 13.3 %all-to-all-done = bf16[32,64,192]{2,1,0:T(8,128)(2,1)} async-done(((bf16[32,64,192]{2,1,0:T(8,128)(2,1)}), bf16[32,64,192]{2,1,0:T(8,128)(2,1)}, u32[]{:S(2)}, u32[]{:S(2)}) %all-to-all-start) | async-done | bytes 786464 | tf_op jit(solution)/shard_map/all_to_all | solution.py:13
  56.1 0.8 dynamic-slice_bitcast_fusion.1
  56.9 0.8 gather_fusion.1
  57.8 5.2 %fusion.12 = f32[16,1,192]{2,1,0:T(1,128)S(1)} fusion(bf16[16,1152,1]{1,2,0:T(2,128)(2,1)S(1)} %reshape.110, bf16[16,192,1152]{2,1,0:T(8,128)(2,1)} %param.14), kind=kOutput, calls=%fused_computation.38 | convolution fusion | flops 7077888 | bytes 7127040 | tf_op jit(solution)/shard_map/bim,bm->bi/dot_general | solution.py:27
  62.9 0.7 fusion.8
  63.9 24.6 %all_gather.7 = bf16[128,192]{1,0:T(8,128)(2,1)S(1)} all-gather(bf16[16,192]{1,0:T(8,128)(2,1)S(1)} %bitcast.59), channel_id=1, replica_groups=mesh['dom'=32,'blk'=8] {'blk'}, dimensions={0}, use_global_device_ids=true | all-gather | bytes 55296 | tf_op jit(solution)/shard_map/all_gather | solution.py:19
  88.5 0.7 gather_fusion.2
  89.2 1.1 broadcast_multiply_fusion
  90.3 5.0 %all-to-all-start.1 = ((bf16[32,64,192]{2,1,0:T(8,128)(2,1)}), bf16[32,64,192]{2,1,0:T(8,128)(2,1)S(1)}, u32[]{:S(2)}, u32[]{:S(2)}) async-start(bf16[32,64,192]{2,1,0:T(8,128)(2,1)} %broadcast_multiply_fusion), calls=%async_computation.1 | async-start | bytes 2097152 | tf_op jit(solution)/shard_map/all_to_all | solution.py:13
  95.5 0.6 dynamic-slice
  96.8 14.8 %all-to-all-done.1 = bf16[32,64,192]{2,1,0:T(8,128)(2,1)S(1)} async-done(((bf16[32,64,192]{2,1,0:T(8,128)(2,1)}), bf16[32,64,192]{2,1,0:T(8,128)(2,1)S(1)}, u32[]{:S(2)}, u32[]{:S(2)}) %all-to-all-start.1) | async-done | bytes 786464 | tf_op jit(solution)/shard_map/all_to_all | solution.py:13
  111.6 0.8 gather_fusion.3
  112.5 5.2 %fusion.13 = f32[16,1,192]{2,1,0:T(1,128)S(1)} fusion(bf16[16,1152,1]{1,2,0:T(2,128)(2,1)S(1)} %reshape.112, bf16[16,192,1152]{2,1,0:T(8,128)(2,1)} %param.14), kind=kOutput, calls=%fused_computation.39 | convolution fusion | flops 7077888 | bytes 7127040 | tf_op jit(solution)/shard_map/bim,bm->bi/dot_general | solution.py:27
  117.7 0.7 fusion.9
  118.7 0.8 gather_fusion.4
  119.8 16.4 %all-reduce = f32[64]{0:T(128)S(1)} all-reduce(f32[64]{0:T(128)S(1)} %fusion), channel_id=2, replica_groups=mesh['dom'=32,'blk'=8] {'blk'}, use_global_device_ids=true, to_apply=%region_1.2.clone | all-reduce | flops 64 | bytes 512
  136.2 0.6 dynamic-slice.1
  (36 shorter events, 1.6 us)
Async XLA Ops:
  31.0 8.9 %copy-start.4 = (s32[16,6]{0,1:T(8,128)S(1)}, s32[16,6]{0,1:T(8,128)}, u32[]{:S(2)}) copy-start(s32[16,6]{0,1:T(8,128)} %param.16) | copy-start | bytes 1156
  31.1 9.7 %copy-start.1 = (bf16[192,3072]{1,0:T(8,128)(2,1)S(1)}, bf16[192,3072]{1,0:T(8,128)(2,1)}, u32[]{:S(2)}) copy-start(bf16[192,3072]{1,0:T(8,128)(2,1)} %param.15) | copy-start | bytes 3538948
  32.2 23.8 %all-to-all-start = ((bf16[32,64,192]{2,1,0:T(8,128)(2,1)}), bf16[32,64,192]{2,1,0:T(8,128)(2,1)}, u32[]{:S(2)}, u32[]{:S(2)}) async-start(bf16[32,64,192]{2,1,0:T(8,128)(2,1)} %broadcast_multiply_fusion.1), calls=%async_computation | async-start | bytes 2097152 | tf_op jit(solution)/shard_map/all_to_all | solution.py:13
  57.8 5.2 %copy-start.3 = (bf16[16,192]{1,0:T(8,128)(2,1)S(1)}, bf16[16,192]{1,0:T(8,128)(2,1)}, u32[]{:S(2)}) copy-start(bf16[16,192]{1,0:T(8,128)(2,1)} %param.12) | copy-start | bytes 18436
  89.2 6.2 %copy-start.2 = (bf16[128,192]{0,1:T(8,128)(2,1)S(1)}, bf16[128,192]{0,1:T(8,128)(2,1)}, u32[]{:S(2)}) copy-start(bf16[128,192]{0,1:T(8,128)(2,1)} %param.21) | copy-start | bytes 147460
  89.2 6.3 %copy-start.7 = (u32[256]{0:T(256)S(1)}, u32[256]{0:T(256)}, u32[]{:S(2)}) copy-start(u32[256]{0:T(256)} %constant.35) | copy-start | bytes 3076
  89.2 7.6 %copy-start.5 = (s32[128]{0:T(128)S(1)}, s32[128]{0:T(128)}, u32[]{:S(2)}) copy-start(s32[128]{0:T(128)} %param.19) | copy-start | bytes 1540
  90.3 21.3 %all-to-all-start.1 = ((bf16[32,64,192]{2,1,0:T(8,128)(2,1)}), bf16[32,64,192]{2,1,0:T(8,128)(2,1)S(1)}, u32[]{:S(2)}, u32[]{:S(2)}) async-start(bf16[32,64,192]{2,1,0:T(8,128)(2,1)} %broadcast_multiply_fusion), calls=%async_computation.1 | async-start | bytes 2097152 | tf_op jit(solution)/shard_map/all_to_all | solution.py:13
  117.7 1.9 %copy-start.6 = (s32[128]{0:T(128)S(1)}, s32[128]{0:T(128)}, u32[]{:S(2)}) copy-start(s32[128]{0:T(128)} %param.20) | copy-start | bytes 1540
  118.7 18.1 %copy-start = (f32[16,1,192]{2,0,1:T(8,128)}, f32[16,1,192]{2,0,1:T(8,128)S(1)}, u32[]{:S(2)}) copy-start(f32[16,1,192]{2,0,1:T(8,128)S(1)} %copy.43) | copy-start | bytes 36868
where the time goes:
time: 137 us
  blocking collectives  69.3 us (51%)
  waiting for transfers between devices  28.1 us (21%)
  starting transfers between devices  12.7 us (9%)
  matrix products  11.1 us (8%)
  local copies, waits for them, and re-layouts  8.15 us (6%)
  other arithmetic  4.47 us (3%)
  between operations  2.83 us (2%)
    all_gather x2, blocking collectives, extended_state(): partition = lax.all_gather(state, 'blk', axis=0, tiled=True)  52.9 us
    all_to_all x2, waiting for transfers between devices, cross_partition(): lax.all_to_all(outgoing, 'dom', split_axis=0, concat_axis=0, tiled=True)  28.1 us
    unnamed x1, blocking collectives  16.4 us
    all_to_all x2, starting transfers between devices, cross_partition(): lax.all_to_all(outgoing, 'dom', split_axis=0, concat_axis=0, tiled=True)  12.7 us
    dot_general x2, matrix products, sweep_once(): jnp.einsum('bim,bm->bi', offd, picked, preferred_element_type=jnp.float32)  10.3 us
  transfers between devices with their start and end apart: 2, of which 2 were waited for; matrix products, arithmetic and copies ran while one was open for 2% of the time, Pallas kernels for 0%

commit v1 on v0

v1 whole, which is shorter than its diff:
```python
import jax
import jax.numpy as jnp
from jax import lax
from jax.experimental import pallas as pl
from jax.experimental.pallas import tpu as pltpu
from jax.sharding import PartitionSpec as P

N_DOM = 32
N_BLK = 8
BD = 16
BW = 192
K = 6
PB = 128
FB = 64
BF = jnp.bfloat16
F32 = jnp.float32


def nt_dot(a, b):
    return lax.dot_general(a, b, (((1,), (1,)), ((), ())), preferred_element_type=F32)


def sweep(z_ref, face_ref, colidx_ref, source_ref, weight_ref, offd_ref, dinv_ref):
    main = z_ref[:, 0:32, :].reshape(N_BLK * 32, 128)
    tails = z_ref[:, 32:48, :].reshape(N_BLK * 16, 128)
    face = face_ref[0, 48:64, :].astype(F32)[0:1, 0:FB]
    columns = colidx_ref[...]
    lane_face = lax.broadcasted_iota(jnp.int32, (BD, FB), 1)
    lane_main = lax.broadcasted_iota(jnp.int32, (BD, N_BLK * 32), 1)
    lane_tail = lax.broadcasted_iota(jnp.int32, (BD, N_BLK * 16), 1)
    hot_main, hot_tail, upper = [], [], []
    for k in range(K):
        c = columns[:, k : k + 1]
        seen = jnp.where(lane_face == c - PB, face, 0.0)
        halo = jnp.sum(seen, axis=1, keepdims=True).astype(jnp.int32)
        other = (c >= PB).astype(jnp.int32)
        block = jnp.where(c >= PB, halo, c)
        dev, row = block // BD, block % BD
        hot_main.append(jnp.where(lane_main == dev * 32 + other * 16 + row, 1.0, 0.0))
        hot_tail.append(jnp.where(lane_tail == dev * 16 + other * 8 + row % 8, 1.0, 0.0))
        upper.append(jnp.broadcast_to(row, (BD, 64)) >= 8)
    got_main = jnp.dot(jnp.concatenate(hot_main, axis=0).astype(BF), main, preferred_element_type=F32)
    got_tail = jnp.dot(jnp.concatenate(hot_tail, axis=0).astype(BF), tails, preferred_element_type=F32)
    pieces = []
    for k in range(K):
        rows = slice(k * BD, (k + 1) * BD)
        tail = got_tail[rows]
        pieces.append(got_main[rows])
        pieces.append(jnp.where(upper[k], tail[:, 64:128], tail[:, 0:64]))
    picked = jnp.concatenate(pieces, axis=1).astype(BF)

    forcing = source_ref[...].astype(F32) * weight_ref[0]
    forcing = jnp.concatenate([forcing, forcing], axis=1)
    row_id = lax.broadcasted_iota(jnp.int32, (BD, 2 * BW), 0)
    half = (lax.broadcasted_iota(jnp.int32, (BD, 2 * BW), 1) >= BW).astype(jnp.int32)
    total = jnp.zeros((BD, BW), F32)
    for pair in range(BD // 2):
        coupling = offd_ref[2 * pair : 2 * pair + 2].reshape(2 * BW, K * BW)
        coupled = nt_dot(picked, coupling)
        rhs = jnp.where(row_id == half + 2 * pair, forcing - coupled, 0.0).astype(BF)
        total = total + nt_dot(rhs, dinv_ref[:, 2 * pair * BW : 2 * (pair + 1) * BW])
    return total


def first_kernel(weight_ref, z_ref, colidx_ref, source_ref, offd_ref, dinv_ref, out_ref):
    total = sweep(z_ref, z_ref, colidx_ref, source_ref, weight_ref, offd_ref, dinv_ref)
    packed = jnp.concatenate(
        [total[:, 0:128], jnp.concatenate([total[0:8, 128:192], total[8:16, 128:192]], axis=1)], axis=0
    )
    out_ref[...] = packed.astype(BF)


def last_kernel(
    weight_ref, z_ref, face_ref, colidx_ref, source_ref, offd_ref, dinv_ref, sens_ref, block_ref, well_ref, adj_ref, sum_ref
):
    total = sweep(z_ref, face_ref, colidx_ref, source_ref, weight_ref, offd_ref, dinv_ref)
    adj_ref[...] = total
    sens = sens_ref[...]
    high = total.astype(BF)
    rest = total - high.astype(F32)
    low = rest.astype(BF)
    lowest = (rest - low.astype(F32)).astype(BF)
    dots = nt_dot(high, sens) + nt_dot(low, sens) + nt_dot(lowest, sens)
    perf = dots.shape[1]
    row_id = lax.broadcasted_iota(jnp.int32, (BD, perf), 0)
    contrib = jnp.sum(jnp.where(row_id == block_ref[...], dots, 0.0), axis=0, keepdims=True)
    well = well_ref[...]
    target = lax.broadcasted_iota(jnp.int32, (N_BLK, perf), 0)
    spread = jnp.where(target == well // 8, -contrib, 0.0)
    lane = lax.broadcasted_iota(jnp.int32, (128, perf), 0)
    hot = jnp.where(lane == well % 8, 1.0, 0.0).astype(BF)
    high = spread.astype(BF)
    rest = spread - high.astype(F32)
    low = rest.astype(BF)
    lowest = (rest - low.astype(F32)).astype(BF)
    sum_ref[...] = nt_dot(high, hot) + nt_dot(low, hot) + nt_dot(lowest, hot)


def pack(rows):
    tails = jnp.concatenate([rows[0:8, 128:192], rows[8:16, 128:192]], axis=1)
    return jnp.concatenate([rows[:, 0:128], tails], axis=0)


def from_partner(message, partner_id):
    sent = jnp.broadcast_to(message[None], (N_DOM,) + message.shape)
    incoming = lax.all_to_all(sent, "dom", split_axis=0, concat_axis=0, tiled=True)
    return lax.dynamic_index_in_dim(incoming, partner_id, 0, keepdims=False)


def to_all(message):
    sent = jnp.broadcast_to(message[None], (N_BLK,) + message.shape)
    return lax.all_to_all(sent, "blk", split_axis=0, concat_axis=0, tiled=True)


def body(
    source,
    lam_init,
    offd,
    dinv,
    colidx,
    face_list,
    partner,
    perf_block,
    perf_well,
    perf_sens,
    obj_weight,
    step_index,
):
    partner_id = partner[0]
    weight = lax.dynamic_slice(obj_weight, (step_index[0],), (1,))
    own = pack(lam_init)
    faces = jnp.pad(face_list.astype(BF), ((0, 7), (0, 64)))
    got = from_partner(jnp.concatenate([own, faces], axis=0), partner_id)
    z1 = to_all(
        jnp.concatenate(
            [own[0:16], got[0:16], own[16:24], got[16:24], got[24:32], jnp.zeros((8, 128), BF)], axis=0
        )
    )
    vmem = pl.BlockSpec(memory_space=pltpu.VMEM)
    smem = pl.BlockSpec(memory_space=pltpu.SMEM)
    limit = pltpu.CompilerParams(vmem_limit_bytes=40 * 1024 * 1024)
    own = pl.pallas_call(
        first_kernel,
        out_shape=jax.ShapeDtypeStruct((24, 128), BF),
        in_specs=[smem] + [vmem] * 5,
        out_specs=vmem,
        compiler_params=limit,
    )(weight, z1, colidx, source, offd, dinv)
    got = from_partner(own, partner_id)
    z2 = to_all(jnp.concatenate([own[0:16], got[0:16], own[16:24], got[16:24]], axis=0))
    perf = perf_block.shape[0]
    adjoint, sums = pl.pallas_call(
        last_kernel,
        out_shape=(jax.ShapeDtypeStruct((BD, BW), F32), jax.ShapeDtypeStruct((N_BLK, 128), F32)),
        in_specs=[smem] + [vmem] * 9,
        out_specs=(vmem, vmem),
        compiler_params=limit,
    )(
        weight,
        z2,
        z1,
        colidx,
        source,
        offd,
        dinv,
        perf_sens,
        perf_block.reshape(1, perf),
        perf_well.reshape(1, perf),
    )
    terms = lax.all_to_all(sums, "blk", split_axis=0, concat_axis=0, tiled=True)
    control_grad = jnp.sum(terms, axis=0)[0:8]
    return (adjoint, control_grad)


def solution(mesh):
    placed = (
        P(("dom", "blk"), None),
        P(("dom", "blk"), None),
        P(("dom", "blk"), None, None),
        P(None, ("dom", "blk")),
        P(("dom", "blk"), None),
        P("dom", None),
        P("dom"),
        P(("dom", "blk")),
        P(("dom", "blk")),
        P(("dom", "blk"), None),
        P(),
        P(),
    )
    return jax.shard_map(
        body,
        mesh=mesh,
        in_specs=placed,
        out_specs=(P(("dom", "blk"), None), P(("dom", "blk"))),
        check_vma=False,
    )
```

time: 137 us -> 91.3 us (0.67)
  blocking collectives: 69.3 us -> 10 us
  starting transfers between devices: 12.7 us -> 24.2 us
  matrix products: 11.1 us -> 0 us
  Pallas kernels: 0 us -> 8.2 us
  local copies, waits for them, and re-layouts: 8.15 us -> 14.5 us
  other arithmetic: 4.47 us -> 1.36 us
  waiting for transfers between devices: 28.1 us -> 30.2 us
    all_gather x2 -> x0, blocking collectives: 52.9 us -> none  [extended_state(): partition = lax.all_gather(state, 'blk', axis=0, tiled=True)]
    unnamed x1 -> x0, blocking collectives: 16.4 us -> none
    all_to_all x2 -> x4, starting transfers between devices: 12.7 us -> 24.2 us  [the longest x2 12.4 us: from_partner(): lax.all_to_all(sent, 'dom', split_axis=0, concat_axis=0, tiled=True)]
    dot_general x5 -> x0, matrix products: 11.1 us -> none  [the longest x2 10.3 us: sweep_once(): jnp.einsum('bim,bm->bi', offd, picked, preferred_element_type=jnp.float32)]
    all_to_all x0 -> x1, blocking collectives: none -> 10 us  [body(): terms = lax.all_to_all(sums, 'blk', split_axis=0, concat_axis=0, tiled=True)]
    pallas_call x0 -> x2, Pallas kernels: none -> 8.2 us  [the longest x1 4.41 us: body(): pl.pallas_call(last_kernel, out_shape=(jax.ShapeDtypeStruct((BD, BW), F32...]
    unnamed x19 -> x23, local copies, waits for them, and re-layouts: 1.32 us -> 8.95 us
    gather x5 -> x0, local copies, waits for them, and re-layouts: 3.71 us -> none  [the longest x2 1.55 us: sweep_once(): picked = extended[colidx].reshape(colidx.shape[0], -1)]
  transfers between devices with their start and end apart: 2 -> 4, of which waited for: 2 -> 4; matrix products, arithmetic and copies ran while one was open for 2% -> 2% of each run, Pallas kernels for 0% -> 0%
where the time goes in v1:
time: 91.3 us; the launch traced here: 90.6 us
  waiting for transfers between devices  30.2 us (33%)
  starting transfers between devices  24.2 us (27%)
  local copies, waits for them, and re-layouts  14.5 us (16%)
  blocking collectives  10 us (11%)
  Pallas kernels  8.2 us (9%)
  between operations  2.07 us (2%)
  other arithmetic  1.36 us (1%)
    all_to_all x2, waiting for transfers between devices, to_all(): return lax.all_to_all(sent, 'blk', split_axis=0, concat_axis=0, tiled=True)  16.1 us
    all_to_all x2, waiting for transfers between devices, from_partner(): lax.all_to_all(sent, 'dom', split_axis=0, concat_axis=0, tiled=True)  14.1 us
    all_to_all x2, starting transfers between devices, from_partner(): lax.all_to_all(sent, 'dom', split_axis=0, concat_axis=0, tiled=True)  12.4 us
    all_to_all x2, starting transfers between devices, to_all(): return lax.all_to_all(sent, 'blk', split_axis=0, concat_axis=0, tiled=True)  11.8 us
    all_to_all x1, blocking collectives, body(): terms = lax.all_to_all(sums, 'blk', split_axis=0, concat_axis=0, tiled=True)  10 us
    unnamed x23, local copies, waits for them, and re-layouts  8.95 us
    pallas_call x1, Pallas kernels, body(): pl.pallas_call(last_kernel, out_shape=(jax.ShapeDtypeStruct((BD, BW), F32...  4.41 us
    pallas_call x1, Pallas kernels, body(): pl.pallas_call(first_kernel, out_shape=jax.ShapeDtypeStruct((24, 128), BF...  3.79 us
  transfers between devices with their start and end apart: 4, of which 4 were waited for; matrix products, arithmetic and copies ran while one was open for 2% of the time, Pallas kernels for 0%

profile of v1, /device:TPU:2, one launch (start us, length us, event | category | flops | bytes accessed | tf_op | source)
XLA Modules:
  0.0 90.6 jit_solution(12539689306211999184)
XLA Ops:
  0.7 0.8 fusion.2
  1.5 0.7 fusion.3
  2.2 0.7 convert_element_type.5
  2.9 0.7 broadcast_in_dim.10
  3.6 7.6 %all-to-all-start = ((bf16[32,32,128]{2,1,0:T(8,128)(2,1)}), bf16[32,32,128]{2,1,0:T(8,128)(2,1)S(1)}, u32[]{:S(2)}, u32[]{:S(2)}) async-start(bf16[32,32,128]{2,1,0:T(8,128)(2,1)} %broadcast_in_dim.10), calls=%async_computation | async-start | bytes 524288 | tf_op jit(solution)/shard_map/all_to_all | solution.py:106
  11.9 7.0 %all-to-all-done = bf16[32,32,128]{2,1,0:T(8,128)(2,1)S(1)} async-done(((bf16[32,32,128]{2,1,0:T(8,128)(2,1)}), bf16[32,32,128]{2,1,0:T(8,128)(2,1)S(1)}, u32[]{:S(2)}, u32[]{:S(2)}) %all-to-all-start) | async-done | bytes 262176 | tf_op jit(solution)/shard_map/all_to_all | solution.py:106
  19.1 0.7 broadcast_in_dim.12
  19.7 8.5 %all-to-all-start.1 = ((bf16[8,64,128]{2,1,0:T(8,128)(2,1)}), bf16[8,64,128]{2,1,0:T(8,128)(2,1)S(1)}, u32[]{:S(2)}, u32[]{:S(2)}) async-start(bf16[8,64,128]{2,1,0:T(8,128)(2,1)} %broadcast_in_dim.12), calls=%async_computation.1 | async-start | bytes 262144 | tf_op jit(solution)/shard_map/all_to_all | solution.py:112
  28.8 0.8 copy.17.colidx_ref
  29.6 1.3 %dynamic_slice.11.weight_ref = f32[1]{0:T(128)} dynamic-slice(f32[1024]{0:T(1024)} %param.22, s32[]{:T(128)S(6)} %select_n.9), dynamic_slice_sizes={1} | dynamic-slice | bytes 12 | tf_op jit(solution)/shard_map/dynamic_slice | solution.py:130
  30.9 7.0 %all-to-all-done.1.z_ref.face_ref = bf16[8,64,128]{2,1,0:T(8,128)(2,1)S(1)} async-done(((bf16[8,64,128]{2,1,0:T(8,128)(2,1)}), bf16[8,64,128]{2,1,0:T(8,128)(2,1)S(1)}, u32[]{:S(2)}, u32[]{:S(2)}) %all-to-all-start.1) | async-done | bytes 131104 | tf_op jit(solution)/shard_map/all_to_all | solution.py:112
  37.9 3.0 %copy-done = bf16[16,192,1152]{2,1,0:T(8,128)(2,1)S(1)} copy-done((bf16[16,192,1152]{2,1,0:T(8,128)(2,1)S(1)}, bf16[16,192,1152]{2,1,0:T(8,128)(2,1)}, u32[]{:S(2)}) %copy-start) | copy-done | bytes 7077912
  40.9 1.3 %copy-done.2 = bf16[192,3072]{1,0:T(8,128)(2,1)S(1)} copy-done((bf16[192,3072]{1,0:T(8,128)(2,1)S(1)}, bf16[192,3072]{1,0:T(8,128)(2,1)}, u32[]{:S(2)}) %copy-start.2) | copy-done | bytes 1179672
  42.2 0.7 copy-done.4
  42.9 3.8 %shard_map.131 = bf16[24,128]{1,0:T(8,128)(2,1)S(1)} custom-call(f32[1]{0:T(128)} %dynamic_slice.11.weight_ref, bf16[8,64,128]{2,1,0:T(8,128)(2,1)S(1)} %all-to-all-done.1.z_ref.face_ref, s32[16,6]{1,0:T(8,128)S(1)} %copy.17.colidx_ref, bf16[16,192]{1,0:T(8,128)(2,1)S(1)} %copy-done.4, bf16[16,192,1152]{2,1,0:T(8,128)(2,1)S(1)} %copy-done, ...), custom_call_target="tpu_custom_call" | custom-call | tf_op jit(solution)/shard_map/pallas_call | solution.py:142
  46.7 0.7 broadcast_in_dim.13
  47.4 4.8 %all-to-all-start.2 = ((bf16[32,24,128]{2,1,0:T(8,128)(2,1)}), bf16[32,24,128]{2,1,0:T(8,128)(2,1)S(1)}, u32[]{:S(2)}, u32[]{:S(2)}) async-start(bf16[32,24,128]{2,1,0:T(8,128)(2,1)} %broadcast_in_dim.13), calls=%async_computation.2 | async-start | bytes 393216 | tf_op jit(solution)/shard_map/all_to_all | solution.py:106
  52.2 7.1 %all-to-all-done.2 = bf16[32,24,128]{2,1,0:T(8,128)(2,1)S(1)} async-done(((bf16[32,24,128]{2,1,0:T(8,128)(2,1)}), bf16[32,24,128]{2,1,0:T(8,128)(2,1)S(1)}, u32[]{:S(2)}, u32[]{:S(2)}) %all-to-all-start.2) | async-done | bytes 196640 | tf_op jit(solution)/shard_map/all_to_all | solution.py:106
  59.3 0.7 broadcast_in_dim.14
  60.0 3.4 %all-to-all-start.3 = ((bf16[8,48,128]{2,1,0:T(8,128)(2,1)}), bf16[8,48,128]{2,1,0:T(8,128)(2,1)S(1)}, u32[]{:S(2)}, u32[]{:S(2)}) async-start(bf16[8,48,128]{2,1,0:T(8,128)(2,1)} %broadcast_in_dim.14), calls=%async_computation.3 | async-start | bytes 196608 | tf_op jit(solution)/shard_map/all_to_all | solution.py:112
  63.5 9.1 %all-to-all-done.3.z_ref = bf16[8,48,128]{2,1,0:T(8,128)(2,1)S(1)} async-done(((bf16[8,48,128]{2,1,0:T(8,128)(2,1)}), bf16[8,48,128]{2,1,0:T(8,128)(2,1)S(1)}, u32[]{:S(2)}, u32[]{:S(2)}) %all-to-all-start.3) | async-done | bytes 98336 | tf_op jit(solution)/shard_map/all_to_all | solution.py:112
  72.6 3.0 %copy-done.1 = bf16[16,192,1152]{2,1,0:T(8,128)(2,1)S(1)} copy-done((bf16[16,192,1152]{2,1,0:T(8,128)(2,1)S(1)}, bf16[16,192,1152]{2,1,0:T(8,128)(2,1)}, u32[]{:S(2)}) %copy-start.1) | copy-done | bytes 7077912
  75.6 4.4 %shard_map.132 = (f32[16,192]{1,0:T(8,128)}, f32[8,128]{1,0:T(8,128)S(1)}) custom-call(f32[1]{0:T(128)} %dynamic_slice.11.weight_ref, bf16[8,48,128]{2,1,0:T(8,128)(2,1)S(1)} %all-to-all-done.3.z_ref, bf16[8,64,128]{2,1,0:T(8,128)(2,1)S(1)} %all-to-all-done.1.z_ref.face_ref, s32[16,6]{1,0:T(8,128)S(1)} %copy.17.colidx_ref, bf16[16,192]{1,0:T(8,128)(2,1)S(1)} %copy-done.5, ...), custom_call_target="tpu_custom_call" | custom-call | tf_op jit(solution)/shard_map/pallas_call | solution.py:152
  80.0 10.0 %all_to_all.29 = f32[8,1,128]{2,1,0:T(1,128)S(1)} all-to-all(f32[8,1,128]{2,1,0:T(1,128)S(1)} %bitcast.30), channel_id=1, replica_groups=mesh['dom'=32,'blk'=8] {'blk'}, dimensions={0} | all-to-all | bytes 8192 | tf_op jit(solution)/shard_map/all_to_all | solution.py:170
  (27 shorter events, 0.9 us)
Async XLA Ops:
  0.6 71.9 %copy-start.5 = (bf16[16,192]{1,0:T(8,128)(2,1)S(1)}, bf16[16,192]{1,0:T(8,128)(2,1)}, u32[]{:S(2)}) copy-start(bf16[16,192]{1,0:T(8,128)(2,1)} %source_ref.3) | copy-start | bytes 18436
  0.6 71.9 %copy-start.3 = (bf16[192,3072]{1,0:T(8,128)(2,1)S(1)}, bf16[192,3072]{1,0:T(8,128)(2,1)}, u32[]{:S(2)}) copy-start(bf16[192,3072]{1,0:T(8,128)(2,1)} %dinv_ref.3) | copy-start | bytes 3538948
  0.7 62.7 %copy-start.8 = (bf16[128,192]{0,1:T(8,128)(2,1)S(1)}, bf16[128,192]{0,1:T(8,128)(2,1)}, u32[]{:S(2)}) copy-start(bf16[128,192]{0,1:T(8,128)(2,1)} %param.21) | copy-start | bytes 147460
  0.7 71.9 %copy-start.6 = (s32[128]{0:T(128)S(1)}, s32[128]{0:T(128)}, u32[]{:S(2)}) copy-start(s32[128]{0:T(128)} %param.19) | copy-start | bytes 1540
  0.7 71.9 %copy-start.7 = (s32[128]{0:T(128)S(1)}, s32[128]{0:T(128)}, u32[]{:S(2)}) copy-start(s32[128]{0:T(128)} %param.20) | copy-start | bytes 1540
  3.6 15.3 %all-to-all-start = ((bf16[32,32,128]{2,1,0:T(8,128)(2,1)}), bf16[32,32,128]{2,1,0:T(8,128)(2,1)S(1)}, u32[]{:S(2)}, u32[]{:S(2)}) async-start(bf16[32,32,128]{2,1,0:T(8,128)(2,1)} %broadcast_in_dim.10), calls=%async_computation | async-start | bytes 524288 | tf_op jit(solution)/shard_map/all_to_all | solution.py:106
  19.7 18.1 %all-to-all-start.1 = ((bf16[8,64,128]{2,1,0:T(8,128)(2,1)}), bf16[8,64,128]{2,1,0:T(8,128)(2,1)S(1)}, u32[]{:S(2)}, u32[]{:S(2)}) async-start(bf16[8,64,128]{2,1,0:T(8,128)(2,1)} %broadcast_in_dim.12), calls=%async_computation.1 | async-start | bytes 262144 | tf_op jit(solution)/shard_map/all_to_all | solution.py:112
  37.9 3.0 %copy-start = (bf16[16,192,1152]{2,1,0:T(8,128)(2,1)S(1)}, bf16[16,192,1152]{2,1,0:T(8,128)(2,1)}, u32[]{:S(2)}) copy-start(bf16[16,192,1152]{2,1,0:T(8,128)(2,1)} %offd_ref.3) | copy-start | bytes 21233668
  40.9 1.3 %copy-start.2 = (bf16[192,3072]{1,0:T(8,128)(2,1)S(1)}, bf16[192,3072]{1,0:T(8,128)(2,1)}, u32[]{:S(2)}) copy-start(bf16[192,3072]{1,0:T(8,128)(2,1)} %dinv_ref.3) | copy-start | bytes 3538948
  42.2 0.7 copy-start.4
  47.4 11.9 %all-to-all-start.2 = ((bf16[32,24,128]{2,1,0:T(8,128)(2,1)}), bf16[32,24,128]{2,1,0:T(8,128)(2,1)S(1)}, u32[]{:S(2)}, u32[]{:S(2)}) async-start(bf16[32,24,128]{2,1,0:T(8,128)(2,1)} %broadcast_in_dim.13), calls=%async_computation.2 | async-start | bytes 393216 | tf_op jit(solution)/shard_map/all_to_all | solution.py:106
  60.0 12.6 %all-to-all-start.3 = ((bf16[8,48,128]{2,1,0:T(8,128)(2,1)}), bf16[8,48,128]{2,1,0:T(8,128)(2,1)S(1)}, u32[]{:S(2)}, u32[]{:S(2)}) async-start(bf16[8,48,128]{2,1,0:T(8,128)(2,1)} %broadcast_in_dim.14), calls=%async_computation.3 | async-start | bytes 196608 | tf_op jit(solution)/shard_map/all_to_all | solution.py:112
  72.5 3.0 %copy-start.1 = (bf16[16,192,1152]{2,1,0:T(8,128)(2,1)S(1)}, bf16[16,192,1152]{2,1,0:T(8,128)(2,1)}, u32[]{:S(2)}) copy-start(bf16[16,192,1152]{2,1,0:T(8,128)(2,1)} %offd_ref.3) | copy-start | bytes 21233668

commit v2 on v1

v2 whole, which is shorter than its diff:
```python
import jax
import jax.numpy as jnp
from jax import lax
from jax.experimental import pallas as pl
from jax.experimental.pallas import tpu as pltpu
from jax.sharding import PartitionSpec as P

N_DOM = 32
N_BLK = 8
BD = 16
BW = 192
K = 6
PB = 128
FB = 64
GROUP = 4
BF = jnp.bfloat16
F32 = jnp.float32


def nt_dot(a, b):
    return lax.dot_general(a, b, (((1,), (1,)), ((), ())), preferred_element_type=F32)


def packed(rows):
    tails = jnp.concatenate([rows[0:8, 128:192], rows[8:16, 128:192]], axis=1)
    return jnp.concatenate([rows[:, 0:128], tails], axis=0)


def three_parts(x):
    high = x.astype(BF)
    rest = x - high.astype(F32)
    mid = rest.astype(BF)
    return high, mid, (rest - mid.astype(F32)).astype(BF)


def entry_kernel(lam_hbm, face_hbm, message_ref, own_ref, lam_ref, face_ref, sems):
    copies = [pltpu.make_async_copy(lam_hbm, lam_ref, sems.at[0]), pltpu.make_async_copy(face_hbm, face_ref, sems.at[1])]
    for copy in copies:
        copy.start()
    for copy in copies:
        copy.wait()
    own = packed(lam_ref[...].astype(F32))
    face = jnp.concatenate([face_ref[...].astype(F32), jnp.zeros((1, 64), F32)], axis=1)
    message = jnp.concatenate([own, jnp.broadcast_to(face, (8, 128))], axis=0).astype(BF)
    own_ref[...] = message
    for slot in range(N_DOM):
        message_ref[slot] = message


def select_kernel(scalars_ref, incoming_ref, own_ref, *refs):
    out_ref = refs[-1]
    got = incoming_ref[jnp.max(scalars_ref[:, 0:1])].astype(F32)
    own = own_ref[...].astype(F32)
    rows = [own[0:16], got[0:16], own[16:24], got[16:24]]
    if out_ref.shape[1] > 48:
        rows.append(got[24:32])
    message = jnp.concatenate(rows, axis=0).astype(BF)
    for slot in range(N_BLK):
        out_ref[slot] = message


def gather_tables(face, columns, main_ref, tail_ref, upper_ref):
    lane_face = lax.broadcasted_iota(jnp.int32, (BD, FB), 1)
    lane_main = lax.broadcasted_iota(jnp.int32, (BD, N_BLK * 32), 1)
    lane_tail = lax.broadcasted_iota(jnp.int32, (BD, N_BLK * 16), 1)
    for k in range(K):
        rows = slice(k * BD, (k + 1) * BD)
        c = columns[:, k : k + 1]
        seen = jnp.where(lane_face == c - PB, face, 0.0)
        halo = jnp.sum(seen, axis=1, keepdims=True).astype(jnp.int32)
        other = (c >= PB).astype(jnp.int32)
        block = jnp.where(c >= PB, halo, c)
        dev, row = block // BD, block % BD
        main_ref[rows, :] = jnp.where(lane_main == dev * 32 + other * 16 + row, 1.0, 0.0).astype(BF)
        tail_ref[rows, :] = jnp.where(lane_tail == dev * 16 + other * 8 + row % 8, 1.0, 0.0).astype(BF)
        upper_ref[rows, :] = jnp.broadcast_to(row // 8, (BD, 64))


def sweep(z_ref, main_ref, tail_ref, upper_ref, forcing, offd, dinv):
    main = z_ref[:, 0:32, :].reshape(N_BLK * 32, 128)
    tails = z_ref[:, 32:48, :].reshape(N_BLK * 16, 128)
    got_main = jnp.dot(main_ref[...], main, preferred_element_type=F32)
    got_tail = jnp.dot(tail_ref[...], tails, preferred_element_type=F32)
    got_tail = jnp.where(upper_ref[...] > 0, got_tail[:, 64:128], got_tail[:, 0:64])
    pieces = []
    for k in range(K):
        rows = slice(k * BD, (k + 1) * BD)
        pieces.append(got_main[rows])
        pieces.append(got_tail[rows])
    picked = jnp.concatenate(pieces, axis=1).astype(BF)

    width = GROUP * BW
    forcing = jnp.concatenate([forcing] * GROUP, axis=1)
    row_id = lax.broadcasted_iota(jnp.int32, (BD, width), 0)
    part = lax.broadcasted_iota(jnp.int32, (BD, width), 1) // BW
    total = jnp.zeros((BD, BW), F32)
    for first in range(0, BD, GROUP):
        coupled = nt_dot(picked, offd[first : first + GROUP].reshape(width, K * BW))
        rhs = jnp.where(row_id == part + first, forcing - coupled, 0.0).astype(BF)
        total = total + nt_dot(rhs, dinv[:, first * BW : (first + GROUP) * BW])
    return total


def first_kernel(
    scalars_ref,
    z_ref,
    columns_ref,
    source_ref,
    weights_ref,
    offd,
    dinv,
    out_ref,
    own_ref,
    forcing_ref,
    main_ref,
    tail_ref,
    upper_ref,
    square,
):
    square[0:K, 0:BD] = columns_ref[...]
    columns = square[...].T[0:BD, :]
    face = z_ref[0].astype(F32)[48:49, 0:FB]
    gather_tables(face, columns, main_ref, tail_ref, upper_ref)
    number = lax.broadcasted_iota(jnp.int32, (8, 128), 0) * 128 + lax.broadcasted_iota(jnp.int32, (8, 128), 1)
    weight = jnp.sum(jnp.where(number == scalars_ref[:, 1:2], weights_ref[...], 0.0), keepdims=True)
    forcing = source_ref[...].astype(F32) * weight
    forcing_ref[...] = forcing
    total = sweep(z_ref, main_ref, tail_ref, upper_ref, forcing, offd, dinv)
    message = packed(total).astype(BF)
    own_ref[...] = message
    for slot in range(N_DOM):
        out_ref[slot] = message


def last_kernel(
    z_ref, main_ref, tail_ref, upper_ref, forcing_ref, sens_ref, block_ref, well_ref, offd, dinv, adj_ref, sum_ref
):
    total = sweep(z_ref, main_ref, tail_ref, upper_ref, forcing_ref[...], offd, dinv)
    adj_ref[...] = total
    sens = sens_ref[...]
    dots = sum(jnp.dot(part, sens, preferred_element_type=F32) for part in three_parts(total))
    perf = dots.shape[1]
    row_id = lax.broadcasted_iota(jnp.int32, (BD, perf), 0)
    contrib = jnp.sum(jnp.where(row_id == block_ref[...], dots, 0.0), axis=0, keepdims=True)
    well = well_ref[...]
    target = lax.broadcasted_iota(jnp.int32, (N_BLK, perf), 0)
    spread = jnp.where(target == well // 8, -contrib, 0.0)
    lane = lax.broadcasted_iota(jnp.int32, (128, perf), 0)
    hot = jnp.where(lane == well % 8, 1.0, 0.0).astype(BF)
    sum_ref[...] = sum(nt_dot(part, hot) for part in three_parts(spread))


def shift(message, axis):
    return lax.all_to_all(message, axis, split_axis=0, concat_axis=0, tiled=True)


def in_hbm(x):
    return pltpu.with_memory_space_constraint(x, pltpu.HBM)


def body(
    source,
    lam_init,
    offd,
    dinv,
    colidx,
    face_list,
    partner,
    perf_block,
    perf_well,
    perf_sens,
    obj_weight,
    step_index,
):
    vmem = pl.BlockSpec(memory_space=pltpu.VMEM)
    hbm = pl.BlockSpec(memory_space=pltpu.HBM)

    def shape(dims, dtype):
        return jax.ShapeDtypeStruct(dims, dtype)

    limit = pltpu.CompilerParams(vmem_limit_bytes=4 * 1024 * 1024)
    small = pltpu.CompilerParams(vmem_limit_bytes=4 * 1024 * 1024)
    message, own = pl.pallas_call(
        entry_kernel,
        out_shape=(shape((N_DOM, 32, 128), BF), shape((32, 128), BF)),
        in_specs=[hbm] * 2,
        out_specs=[vmem] * 2,
        scratch_shapes=[pltpu.VMEM((BD, BW), BF), pltpu.VMEM((1, FB), jnp.int32), pltpu.SemaphoreType.DMA((2,))],
        compiler_params=small,
    )(in_hbm(lam_init), in_hbm(face_list))
    scalars = jnp.concatenate([partner, step_index]).reshape(1, 2)

    def spread(incoming, own, rows, *unread):
        return pl.pallas_call(
            select_kernel,
            out_shape=shape((N_BLK, rows, 128), BF),
            in_specs=[vmem] * 3 + [hbm] * len(unread),
            out_specs=vmem,
            compiler_params=small,
        )(scalars, incoming, own, *unread)

    z1 = shift(spread(shift(message, "dom"), own, 56, in_hbm(offd), in_hbm(dinv)), "blk")
    message, own, forcing, *tables = pl.pallas_call(
        first_kernel,
        out_shape=(
            shape((N_DOM, 24, 128), BF),
            shape((24, 128), BF),
            shape((BD, BW), F32),
            shape((K * BD, N_BLK * 32), BF),
            shape((K * BD, N_BLK * 16), BF),
            shape((K * BD, 64), jnp.int32),
        ),
        in_specs=[vmem] * 7,
        out_specs=[vmem] * 6,
        scratch_shapes=[pltpu.VMEM((128, 128), jnp.int32)],
        compiler_params=limit,
    )(scalars, z1, colidx.T, source, obj_weight.reshape(8, 128), offd, dinv)
    z2 = shift(spread(shift(message, "dom"), own, 48), "blk")
    perf = perf_block.shape[0]
    adjoint, sums = pl.pallas_call(
        last_kernel,
        out_shape=(shape((BD, BW), F32), shape((N_BLK, 128), F32)),
        in_specs=[vmem] * 10,
        out_specs=(vmem, vmem),
        compiler_params=limit,
    )(
        z2,
        *tables,
        forcing,
        perf_sens.T,
        perf_block.reshape(1, perf),
        perf_well.reshape(1, perf),
        offd,
        dinv,
    )
    control_grad = jnp.sum(shift(sums, "blk"), axis=0)[0:8]
    return (adjoint, control_grad)


def solution(mesh):
    placed = (
        P(("dom", "blk"), None),
        P(("dom", "blk"), None),
        P(("dom", "blk"), None, None),
        P(None, ("dom", "blk")),
        P(("dom", "blk"), None),
        P("dom", None),
        P("dom"),
        P(("dom", "blk")),
        P(("dom", "blk")),
        P(("dom", "blk"), None),
        P(),
        P(),
    )
    return jax.shard_map(
        body,
        mesh=mesh,
        in_specs=placed,
        out_specs=(P(("dom", "blk"), None), P(("dom", "blk"))),
        check_vma=False,
    )
```

time: 91.3 us -> 75.9 us (0.83)
  blocking collectives: 10 us -> 51.1 us
  waiting for transfers between devices: 30.2 us -> 6.32 us
  starting transfers between devices: 24.2 us -> 7.63 us
  local copies, waits for them, and re-layouts: 14.5 us -> 0.03 us
    all_to_all x1 -> x4, blocking collectives: 10 us -> 51.1 us  [shift(): lax.all_to_all(message, axis, split_axis=0, concat_axis=0, tiled=True)]
    all_to_all x4 -> x1, waiting for transfers between devices: 30.2 us -> 6.32 us  [shift(): lax.all_to_all(message, axis, split_axis=0, concat_axis=0, tiled=True)]
    all_to_all x4 -> x1, starting transfers between devices: 24.2 us -> 7.63 us  [shift(): lax.all_to_all(message, axis, split_axis=0, concat_axis=0, tiled=True)]
    unnamed x23 -> x16, local copies, waits for them, and re-layouts: 8.95 us -> 0.03 us
    broadcast_in_dim x4 -> x0, local copies, waits for them, and re-layouts: 2.79 us -> none  [the longest x2 1.45 us: from_partner(): sent = jnp.broadcast_to(message[None], (N_DOM,) + message.shape)]
    slice x6 -> x0, local copies, waits for them, and re-layouts: 1.49 us -> none  [the longest x1 0.78 us: pack(): return jnp.concatenate([rows[:, 0:128], tails], axis=0)]
    dynamic_slice x1 -> x0, local copies, waits for them, and re-layouts: 1.27 us -> none  [body(): weight = lax.dynamic_slice(obj_weight, (step_index[0],), (1,))]
    pallas_call x2 -> x5, Pallas kernels: 8.2 us -> 7.89 us  [the longest x1 3.18 us: body(): pl.pallas_call(last_kernel, out_shape=(shape((BD, BW), F32), shape((N_BLK...]
  transfers between devices with their start and end apart: 4 -> 1, of which waited for: 4 -> 1; matrix products, arithmetic and copies ran while one was open for 2% -> 0% of each run, Pallas kernels for 0% -> 0%
where the time goes in v2:
time: 75.9 us; the launch traced here: 75.6 us
  blocking collectives  51.1 us (67%)
  Pallas kernels  7.89 us (10%)
  starting transfers between devices  7.63 us (10%)
  waiting for transfers between devices  6.32 us (8%)
  between operations  2.03 us (3%)
    all_to_all x4, blocking collectives, shift(): lax.all_to_all(message, axis, split_axis=0, concat_axis=0, tiled=True)  51.1 us
    all_to_all x1, starting transfers between devices, shift(): lax.all_to_all(message, axis, split_axis=0, concat_axis=0, tiled=True)  7.63 us
    all_to_all x1, waiting for transfers between devices, shift(): lax.all_to_all(message, axis, split_axis=0, concat_axis=0, tiled=True)  6.32 us
    pallas_call x1, Pallas kernels, body(): pl.pallas_call(last_kernel, out_shape=(shape((BD, BW), F32), shape((N_BLK...  3.18 us
    pallas_call x1, Pallas kernels, body(): pl.pallas_call(first_kernel, out_shape=(shape((N_DOM, 24, 128), BF), shap...  3.02 us
    pallas_call x1, Pallas kernels, body(): pl.pallas_call(entry_kernel, out_shape=(shape((N_DOM, 32, 128), BF), shap...  1.59 us
  transfers between devices with their start and end apart: 1, of which 1 were waited for; matrix products, arithmetic and copies ran while one was open for 0% of the time, Pallas kernels for 0%

profile of v2, /device:TPU:2, one launch (start us, length us, event | category | flops | bytes accessed | tf_op | source)
XLA Modules:
  0.0 75.6 jit_solution(10341187538805749138)
XLA Ops:
  0.6 0.0 copy-start.1
  0.6 0.0 copy-start.5
  0.7 0.0 copy-start.4
  0.7 0.0 copy-start.3
  0.7 1.6 %shard_map.131 = (bf16[32,32,128]{2,1,0:T(8,128)(2,1)}, bf16[32,128]{1,0:T(8,128)(2,1)S(1)}) custom-call(bf16[16,192]{1,0:T(8,128)(2,1)} %lam_hbm.1, s32[1,64]{1,0:T(1,128)} %face_hbm.1), custom_call_target="tpu_custom_call" | custom-call | tf_op jit(solution)/shard_map/pallas_call | solution.py:183
  2.3 7.6 %all-to-all-start = ((bf16[32,32,128]{2,1,0:T(8,128)(2,1)}), bf16[32,32,128]{2,1,0:T(8,128)(2,1)S(1)}, u32[]{:S(2)}, u32[]{:S(2)}) async-start(bf16[32,32,128]{2,1,0:T(8,128)(2,1)} %get-tuple-element.12), calls=%async_computation | async-start | bytes 524288 | tf_op jit(solution)/shard_map/all_to_all | solution.py:154
  11.2 0.1 add_bitcast_fusion.scalars_ref
  11.3 6.3 %all-to-all-done.incoming_ref = bf16[32,32,128]{2,1,0:T(8,128)(2,1)S(1)} async-done(((bf16[32,32,128]{2,1,0:T(8,128)(2,1)}), bf16[32,32,128]{2,1,0:T(8,128)(2,1)S(1)}, u32[]{:S(2)}, u32[]{:S(2)}) %all-to-all-start) | async-done | bytes 262176 | tf_op jit(solution)/shard_map/all_to_all | solution.py:154
  17.6 0.0 copy-start
  17.7 17.9 %all_to_all.29.z_ref = bf16[8,56,128]{2,1,0:T(8,128)(2,1)S(1)} all-to-all(bf16[8,56,128]{2,1,0:T(8,128)(2,1)S(1)} %shard_map.132), channel_id=1, replica_groups=mesh['dom'=32,'blk'=8] {'blk'}, dimensions={0} | all-to-all | bytes 229376 | tf_op jit(solution)/shard_map/all_to_all | solution.py:154
  35.5 0.0 copy-done.1
  35.5 0.0 copy-done.5
  35.5 0.0 copy-done.4
  35.5 0.0 copy-done.3
  35.5 0.0 copy-done
  35.6 3.0 %shard_map.133 = (bf16[32,24,128]{2,1,0:T(8,128)(2,1)S(1)}, bf16[24,128]{1,0:T(8,128)(2,1)S(1)}, f32[16,192]{1,0:T(8,128)S(1)}, bf16[96,256]{1,0:T(8,128)(2,1)S(...) custom-call(s32[1,2]{1,0:T(1,128)S(1)} %add_bitcast_fusion.scalars_ref, bf16[8,56,128]{2,1,0:T(8,128)(2,1)S(1)} %all_to_all.29.z_ref, ...), custom_call_target="tpu_custom_call" | custom-call | tf_op jit(solution)/shard_map/pallas_call | solution.py:203
  38.6 11.5 %all_to_all.30.incoming_ref = bf16[32,24,128]{2,1,0:T(8,128)(2,1)S(1)} all-to-all(bf16[32,24,128]{2,1,0:T(8,128)(2,1)S(1)} %get-tuple-element.14), channel_id=1, replica_groups=mesh['dom'=32,'blk'=8] {'dom'}, dimensions={0} | all-to-all | bytes 393216 | tf_op jit(solution)/shard_map/all_to_all | solution.py:154
  50.2 11.7 %all_to_all.31.z_ref = bf16[8,48,128]{2,1,0:T(8,128)(2,1)S(1)} all-to-all(bf16[8,48,128]{2,1,0:T(8,128)(2,1)S(1)} %shard_map.134), channel_id=1, replica_groups=mesh['dom'=32,'blk'=8] {'blk'}, dimensions={0} | all-to-all | bytes 196608 | tf_op jit(solution)/shard_map/all_to_all | solution.py:154
  61.8 0.0 copy-done.2
  61.8 0.0 copy-done.6
  61.8 0.0 copy-done.7
  61.8 3.2 %shard_map.135 = (f32[16,192]{1,0:T(8,128)}, f32[8,128]{1,0:T(8,128)S(1)}) custom-call(bf16[8,48,128]{2,1,0:T(8,128)(2,1)S(1)} %all_to_all.31.z_ref, bf16[96,256]{1,0:T(8,128)(2,1)S(1)} %get-tuple-element.16.main_ref, bf16[96,128]{1,0:T(8,128)(2,1)S(1)} %get-tuple-element.17.tail_ref, s32[96,64]{1,0:T(8,128)S(1)} %get-tuple-element.18.upper_ref, ...), custom_call_target="tpu_custom_call" | custom-call | tf_op jit(solution)/shard_map/pallas_call | solution.py:220
  65.0 10.0 %all_to_all.32 = f32[8,1,128]{2,1,0:T(1,128)S(1)} all-to-all(f32[8,1,128]{2,1,0:T(1,128)S(1)} %bitcast.14), channel_id=1, replica_groups=mesh['dom'=32,'blk'=8] {'blk'}, dimensions={0} | all-to-all | bytes 8192 | tf_op jit(solution)/shard_map/all_to_all | solution.py:154
  75.0 0.5 reduce_sum.9
  (5 shorter events, 0.1 us)
Async XLA Ops:
  0.6 34.9 %copy-start.1 = (bf16[192,3072]{1,0:T(8,128)(2,1)S(1)}, bf16[192,3072]{1,0:T(8,128)(2,1)}, u32[]{:S(2)}) copy-start(bf16[192,3072]{1,0:T(8,128)(2,1)} %dinv.3) | copy-start | bytes 3538948
  0.6 34.9 %copy-start.5 = (f32[1024]{0:T(1024)S(1)}, f32[1024]{0:T(1024)}, u32[]{:S(2)}) copy-start(f32[1024]{0:T(1024)} %param.22) | copy-start | bytes 12292
  0.7 34.9 %copy-start.4 = (s32[16,6]{0,1:T(8,128)S(1)}, s32[16,6]{0,1:T(8,128)}, u32[]{:S(2)}) copy-start(s32[16,6]{0,1:T(8,128)} %param.16) | copy-start | bytes 1156
  0.7 34.9 %copy-start.3 = (bf16[16,192]{1,0:T(8,128)(2,1)S(1)}, bf16[16,192]{1,0:T(8,128)(2,1)}, u32[]{:S(2)}) copy-start(bf16[16,192]{1,0:T(8,128)(2,1)} %source_ref.1) | copy-start | bytes 18436
  2.3 15.3 %all-to-all-start = ((bf16[32,32,128]{2,1,0:T(8,128)(2,1)}), bf16[32,32,128]{2,1,0:T(8,128)(2,1)S(1)}, u32[]{:S(2)}, u32[]{:S(2)}) async-start(bf16[32,32,128]{2,1,0:T(8,128)(2,1)} %get-tuple-element.12), calls=%async_computation | async-start | bytes 524288 | tf_op jit(solution)/shard_map/all_to_all | solution.py:154
  17.6 17.9 %copy-start = (bf16[16,192,1152]{2,1,0:T(8,128)(2,1)S(1)}, bf16[16,192,1152]{2,1,0:T(8,128)(2,1)}, u32[]{:S(2)}) copy-start(bf16[16,192,1152]{2,1,0:T(8,128)(2,1)} %offd.3) | copy-start | bytes 21233668
  17.6 44.2 %copy-start.2 = (bf16[128,192]{0,1:T(8,128)(2,1)S(1)}, bf16[128,192]{0,1:T(8,128)(2,1)}, u32[]{:S(2)}) copy-start(bf16[128,192]{0,1:T(8,128)(2,1)} %param.21) | copy-start | bytes 147460
  17.6 44.2 %copy-start.6 = (s32[128]{0:T(128)S(1)}, s32[128]{0:T(128)}, u32[]{:S(2)}) copy-start(s32[128]{0:T(128)} %param.19) | copy-start | bytes 1540
  17.6 44.2 %copy-start.7 = (s32[128]{0:T(128)S(1)}, s32[128]{0:T(128)}, u32[]{:S(2)}) copy-start(s32[128]{0:T(128)} %param.20) | copy-start | bytes 1540

commit v3 on v2

--- a/solution.py
+++ b/solution.py
@@ -152,6 +152,12 @@
 
 def shift(message, axis):
     return lax.all_to_all(message, axis, split_axis=0, concat_axis=0, tiled=True)
+
+
+def result_kernel(terms_ref, total_ref, adj_ref, grad_ref):
+    adj_ref[...] = total_ref[...]
+    terms = terms_ref[:, 0, :]
+    grad_ref[...] = jnp.sum(terms, axis=0, keepdims=True)[:, 0:8]
 
 
 def in_hbm(x):
@@ -233,8 +239,15 @@
         offd,
         dinv,
     )
-    control_grad = jnp.sum(shift(sums, "blk"), axis=0)[0:8]
-    return (adjoint, control_grad)
+    terms = shift(sums.reshape(N_BLK, 1, 128), "blk")
+    adjoint, control_grad = pl.pallas_call(
+        result_kernel,
+        out_shape=(shape((BD, BW), F32), shape((1, 8), F32)),
+        in_specs=[vmem] * 2,
+        out_specs=(vmem, vmem),
+        compiler_params=small,
+    )(terms, adjoint)
+    return (adjoint, control_grad.reshape(8))
 
 
 def solution(mesh):

time: 75.9 us -> 75.7 us (level)
  no operation moved by 1% of the time
where the time goes in v3:
time: 75.7 us; the launch traced here: 75.3 us
  blocking collectives  51.1 us (68%)
  Pallas kernels  8.16 us (11%)
  starting transfers between devices  7.63 us (10%)
  waiting for transfers between devices  6.32 us (8%)
  between operations  2.03 us (3%)
    all_to_all x4, blocking collectives, shift(): lax.all_to_all(message, axis, split_axis=0, concat_axis=0, tiled=True)  51.1 us
    all_to_all x1, starting transfers between devices, shift(): lax.all_to_all(message, axis, split_axis=0, concat_axis=0, tiled=True)  7.63 us
    all_to_all x1, waiting for transfers between devices, shift(): lax.all_to_all(message, axis, split_axis=0, concat_axis=0, tiled=True)  6.32 us
    pallas_call x1, Pallas kernels, body(): pl.pallas_call(first_kernel, out_shape=(shape((N_DOM, 24, 128), BF), shap...  3.02 us
    pallas_call x1, Pallas kernels, body(): pl.pallas_call(last_kernel, out_shape=(shape((BD, BW), F32), shape((N_BLK...  2.86 us
    pallas_call x1, Pallas kernels, body(): pl.pallas_call(entry_kernel, out_shape=(shape((N_DOM, 32, 128), BF), shap...  1.58 us
  transfers between devices with their start and end apart: 1, of which 1 were waited for; matrix products, arithmetic and copies ran while one was open for 0% of the time, Pallas kernels for 0%

profile of v3, /device:TPU:2, one launch (start us, length us, event | category | flops | bytes accessed | tf_op | source)
XLA Modules:
  0.0 75.3 jit_solution(13044958642687769514)
XLA Ops:
  0.6 0.0 copy-start.1
  0.6 0.0 copy-start.5
  0.7 0.0 copy-start.4
  0.7 0.0 copy-start.3
  0.7 1.6 %shard_map.131 = (bf16[32,32,128]{2,1,0:T(8,128)(2,1)}, bf16[32,128]{1,0:T(8,128)(2,1)S(1)}) custom-call(bf16[16,192]{1,0:T(8,128)(2,1)} %lam_hbm.1, s32[1,64]{1,0:T(1,128)} %face_hbm.1), custom_call_target="tpu_custom_call" | custom-call | tf_op jit(solution)/shard_map/pallas_call | solution.py:189
  2.3 7.6 %all-to-all-start = ((bf16[32,32,128]{2,1,0:T(8,128)(2,1)}), bf16[32,32,128]{2,1,0:T(8,128)(2,1)S(1)}, u32[]{:S(2)}, u32[]{:S(2)}) async-start(bf16[32,32,128]{2,1,0:T(8,128)(2,1)} %get-tuple-element.14), calls=%async_computation | async-start | bytes 524288 | tf_op jit(solution)/shard_map/all_to_all | solution.py:154
  11.2 0.1 add_bitcast_fusion.scalars_ref
  11.3 6.3 %all-to-all-done.incoming_ref = bf16[32,32,128]{2,1,0:T(8,128)(2,1)S(1)} async-done(((bf16[32,32,128]{2,1,0:T(8,128)(2,1)}), bf16[32,32,128]{2,1,0:T(8,128)(2,1)S(1)}, u32[]{:S(2)}, u32[]{:S(2)}) %all-to-all-start) | async-done | bytes 262176 | tf_op jit(solution)/shard_map/all_to_all | solution.py:154
  17.6 0.0 copy-start
  17.6 17.9 %all_to_all.25.z_ref = bf16[8,56,128]{2,1,0:T(8,128)(2,1)S(1)} all-to-all(bf16[8,56,128]{2,1,0:T(8,128)(2,1)S(1)} %shard_map.132), channel_id=1, replica_groups=mesh['dom'=32,'blk'=8] {'blk'}, dimensions={0} | all-to-all | bytes 229376 | tf_op jit(solution)/shard_map/all_to_all | solution.py:154
  35.5 0.0 copy-done.1
  35.5 0.0 copy-done.5
  35.5 0.0 copy-done.4
  35.5 0.0 copy-done.3
  35.5 0.0 copy-done
  35.5 3.0 %shard_map.133 = (bf16[32,24,128]{2,1,0:T(8,128)(2,1)S(1)}, bf16[24,128]{1,0:T(8,128)(2,1)S(1)}, f32[16,192]{1,0:T(8,128)S(1)}, bf16[96,256]{1,0:T(8,128)(2,1)S(...) custom-call(s32[1,2]{1,0:T(1,128)S(1)} %add_bitcast_fusion.scalars_ref, bf16[8,56,128]{2,1,0:T(8,128)(2,1)S(1)} %all_to_all.25.z_ref, ...), custom_call_target="tpu_custom_call" | custom-call | tf_op jit(solution)/shard_map/pallas_call | solution.py:209
  38.6 11.5 %all_to_all.26.incoming_ref = bf16[32,24,128]{2,1,0:T(8,128)(2,1)S(1)} all-to-all(bf16[32,24,128]{2,1,0:T(8,128)(2,1)S(1)} %get-tuple-element.16), channel_id=1, replica_groups=mesh['dom'=32,'blk'=8] {'dom'}, dimensions={0} | all-to-all | bytes 393216 | tf_op jit(solution)/shard_map/all_to_all | solution.py:154
  50.1 11.7 %all_to_all.27.z_ref = bf16[8,48,128]{2,1,0:T(8,128)(2,1)S(1)} all-to-all(bf16[8,48,128]{2,1,0:T(8,128)(2,1)S(1)} %shard_map.134), channel_id=1, replica_groups=mesh['dom'=32,'blk'=8] {'blk'}, dimensions={0} | all-to-all | bytes 196608 | tf_op jit(solution)/shard_map/all_to_all | solution.py:154
  61.8 0.0 copy-done.2
  61.8 0.0 copy-done.6
  61.8 0.0 copy-done.7
  61.8 2.9 %shard_map.135 = (f32[16,192]{1,0:T(8,128)S(1)}, f32[8,128]{1,0:T(8,128)S(1)}) custom-call(bf16[8,48,128]{2,1,0:T(8,128)(2,1)S(1)} %all_to_all.27.z_ref, bf16[96,256]{1,0:T(8,128)(2,1)S(1)} %get-tuple-element.18.main_ref, bf16[96,128]{1,0:T(8,128)(2,1)S(1)} %get-tuple-element.19.tail_ref, s32[96,64]{1,0:T(8,128)S(1)} %get-tuple-element.20.upper_ref, ...), custom_call_target="tpu_custom_call" | custom-call | tf_op jit(solution)/shard_map/pallas_call | solution.py:226
  64.7 10.1 %all_to_all.28.terms_ref = f32[8,1,128]{2,1,0:T(1,128)S(1)} all-to-all(f32[8,1,128]{2,1,0:T(1,128)S(1)} %bitcast.12), channel_id=1, replica_groups=mesh['dom'=32,'blk'=8] {'blk'}, dimensions={0} | all-to-all | bytes 8192 | tf_op jit(solution)/shard_map/all_to_all | solution.py:154
  74.7 0.6 shard_map.136
  (5 shorter events, 0.1 us)
Async XLA Ops:
  0.6 34.9 %copy-start.1 = (bf16[192,3072]{1,0:T(8,128)(2,1)S(1)}, bf16[192,3072]{1,0:T(8,128)(2,1)}, u32[]{:S(2)}) copy-start(bf16[192,3072]{1,0:T(8,128)(2,1)} %dinv.3) | copy-start | bytes 3538948
  0.6 34.9 %copy-start.5 = (f32[1024]{0:T(1024)S(1)}, f32[1024]{0:T(1024)}, u32[]{:S(2)}) copy-start(f32[1024]{0:T(1024)} %param.22) | copy-start | bytes 12292
  0.7 34.9 %copy-start.4 = (s32[16,6]{0,1:T(8,128)S(1)}, s32[16,6]{0,1:T(8,128)}, u32[]{:S(2)}) copy-start(s32[16,6]{0,1:T(8,128)} %param.16) | copy-start | bytes 1156
  0.7 34.9 %copy-start.3 = (bf16[16,192]{1,0:T(8,128)(2,1)S(1)}, bf16[16,192]{1,0:T(8,128)(2,1)}, u32[]{:S(2)}) copy-start(bf16[16,192]{1,0:T(8,128)(2,1)} %source_ref.1) | copy-start | bytes 18436
  2.3 15.3 %all-to-all-start = ((bf16[32,32,128]{2,1,0:T(8,128)(2,1)}), bf16[32,32,128]{2,1,0:T(8,128)(2,1)S(1)}, u32[]{:S(2)}, u32[]{:S(2)}) async-start(bf16[32,32,128]{2,1,0:T(8,128)(2,1)} %get-tuple-element.14), calls=%async_computation | async-start | bytes 524288 | tf_op jit(solution)/shard_map/all_to_all | solution.py:154
  17.6 17.9 %copy-start = (bf16[16,192,1152]{2,1,0:T(8,128)(2,1)S(1)}, bf16[16,192,1152]{2,1,0:T(8,128)(2,1)}, u32[]{:S(2)}) copy-start(bf16[16,192,1152]{2,1,0:T(8,128)(2,1)} %offd.3) | copy-start | bytes 21233668
  17.6 44.2 %copy-start.2 = (bf16[128,192]{0,1:T(8,128)(2,1)S(1)}, bf16[128,192]{0,1:T(8,128)(2,1)}, u32[]{:S(2)}) copy-start(bf16[128,192]{0,1:T(8,128)(2,1)} %param.21) | copy-start | bytes 147460
  17.6 44.2 %copy-start.6 = (s32[128]{0:T(128)S(1)}, s32[128]{0:T(128)}, u32[]{:S(2)}) copy-start(s32[128]{0:T(128)} %param.19) | copy-start | bytes 1540
  17.6 44.2 %copy-start.7 = (s32[128]{0:T(128)S(1)}, s32[128]{0:T(128)}, u32[]{:S(2)}) copy-start(s32[128]{0:T(128)} %param.20) | copy-start | bytes 1540

commit v4 on v3

--- a/solution.py
+++ b/solution.py
@@ -82,20 +82,33 @@
     got_main = jnp.dot(main_ref[...], main, preferred_element_type=F32)
     got_tail = jnp.dot(tail_ref[...], tails, preferred_element_type=F32)
     got_tail = jnp.where(upper_ref[...] > 0, got_tail[:, 64:128], got_tail[:, 0:64])
-    pieces = []
-    for k in range(K):
-        rows = slice(k * BD, (k + 1) * BD)
-        pieces.append(got_main[rows])
-        pieces.append(got_tail[rows])
-    picked = jnp.concatenate(pieces, axis=1).astype(BF)
-
     width = GROUP * BW
     forcing = jnp.concatenate([forcing] * GROUP, axis=1)
     row_id = lax.broadcasted_iota(jnp.int32, (BD, width), 0)
     part = lax.broadcasted_iota(jnp.int32, (BD, width), 1) // BW
+    pieces = []
+    for pair in range(K // 2):
+        first, second = (slice(k * BD, (k + 1) * BD) for k in (2 * pair, 2 * pair + 1))
+        pieces.append(got_main[first])
+        pieces.append(jnp.concatenate([got_tail[first], got_main[second][:, 0:64]], axis=1))
+        pieces.append(jnp.concatenate([got_main[second][:, 64:128], got_tail[second]], axis=1))
+    ones = jnp.ones((BD, 128), BF)
     total = jnp.zeros((BD, BW), F32)
     for first in range(0, BD, GROUP):
-        coupled = nt_dot(picked, offd[first : first + GROUP].reshape(width, K * BW))
+        coupled = []
+        for block in range(first, first + GROUP):
+            factors = [jnp.broadcast_to(piece[block : block + 1, :], (16, 128)) for piece in pieces]
+            lanes = []
+            for row in range(0, BW, 16):
+                partial = None
+                for tile, factor in enumerate(factors):
+                    term = offd[block, row : row + 16, tile * 128 : (tile + 1) * 128].astype(F32) * factor
+                    partial = term if partial is None else partial + term
+                lanes.append(partial)
+            lanes = jnp.concatenate(lanes, axis=0)
+            high = lanes.astype(BF)
+            coupled.append(nt_dot(ones, high) + nt_dot(ones, (lanes - high.astype(F32)).astype(BF)))
+        coupled = jnp.concatenate(coupled, axis=1)
         rhs = jnp.where(row_id == part + first, forcing - coupled, 0.0).astype(BF)
         total = total + nt_dot(rhs, dinv[:, first * BW : (first + GROUP) * BW])
     return total

time: 75.7 us -> 74.9 us (0.989)
  no operation moved by 1% of the time
where the time goes in v4:
time: 74.9 us; the launch traced here: 74.6 us
  blocking collectives  51.1 us (68%)
  starting transfers between devices  7.63 us (10%)
  Pallas kernels  7.41 us (10%)
  waiting for transfers between devices  6.32 us (8%)
  between operations  2.03 us (3%)
    all_to_all x4, blocking collectives, shift(): lax.all_to_all(message, axis, split_axis=0, concat_axis=0, tiled=True)  51.1 us
    all_to_all x1, starting transfers between devices, shift(): lax.all_to_all(message, axis, split_axis=0, concat_axis=0, tiled=True)  7.63 us
    all_to_all x1, waiting for transfers between devices, shift(): lax.all_to_all(message, axis, split_axis=0, concat_axis=0, tiled=True)  6.32 us
    pallas_call x1, Pallas kernels, body(): pl.pallas_call(first_kernel, out_shape=(shape((N_DOM, 24, 128), BF), shap...  2.62 us
    pallas_call x1, Pallas kernels, body(): pl.pallas_call(last_kernel, out_shape=(shape((BD, BW), F32), shape((N_BLK...  2.51 us
    pallas_call x1, Pallas kernels, body(): pl.pallas_call(entry_kernel, out_shape=(shape((N_DOM, 32, 128), BF), shap...  1.58 us
  transfers between devices with their start and end apart: 1, of which 1 were waited for; matrix products, arithmetic and copies ran while one was open for 0% of the time, Pallas kernels for 0%

profile of v4, /device:TPU:2, one launch (start us, length us, event | category | flops | bytes accessed | tf_op | source)
XLA Modules:
  0.0 74.6 jit_solution(18306975828651109965)
XLA Ops:
  0.6 0.0 copy-start.1
  0.6 0.0 copy-start.5
  0.7 0.0 copy-start.4
  0.7 0.0 copy-start.3
  0.7 1.6 %shard_map.131 = (bf16[32,32,128]{2,1,0:T(8,128)(2,1)}, bf16[32,128]{1,0:T(8,128)(2,1)S(1)}) custom-call(bf16[16,192]{1,0:T(8,128)(2,1)} %lam_hbm.1, s32[1,64]{1,0:T(1,128)} %face_hbm.1), custom_call_target="tpu_custom_call" | custom-call | tf_op jit(solution)/shard_map/pallas_call | solution.py:202
  2.3 7.6 %all-to-all-start = ((bf16[32,32,128]{2,1,0:T(8,128)(2,1)}), bf16[32,32,128]{2,1,0:T(8,128)(2,1)S(1)}, u32[]{:S(2)}, u32[]{:S(2)}) async-start(bf16[32,32,128]{2,1,0:T(8,128)(2,1)} %get-tuple-element.14), calls=%async_computation | async-start | bytes 524288 | tf_op jit(solution)/shard_map/all_to_all | solution.py:167
  11.2 0.1 add_bitcast_fusion.scalars_ref
  11.3 6.3 %all-to-all-done.incoming_ref = bf16[32,32,128]{2,1,0:T(8,128)(2,1)S(1)} async-done(((bf16[32,32,128]{2,1,0:T(8,128)(2,1)}), bf16[32,32,128]{2,1,0:T(8,128)(2,1)S(1)}, u32[]{:S(2)}, u32[]{:S(2)}) %all-to-all-start) | async-done | bytes 262176 | tf_op jit(solution)/shard_map/all_to_all | solution.py:167
  17.6 0.0 copy-start
  17.6 17.9 %all_to_all.25.z_ref = bf16[8,56,128]{2,1,0:T(8,128)(2,1)S(1)} all-to-all(bf16[8,56,128]{2,1,0:T(8,128)(2,1)S(1)} %shard_map.132), channel_id=1, replica_groups=mesh['dom'=32,'blk'=8] {'blk'}, dimensions={0} | all-to-all | bytes 229376 | tf_op jit(solution)/shard_map/all_to_all | solution.py:167
  35.5 0.0 copy-done.1
  35.5 0.0 copy-done.5
  35.5 0.0 copy-done.4
  35.5 0.0 copy-done.3
  35.5 0.0 copy-done
  35.5 2.6 %shard_map.133 = (bf16[32,24,128]{2,1,0:T(8,128)(2,1)S(1)}, bf16[24,128]{1,0:T(8,128)(2,1)S(1)}, f32[16,192]{1,0:T(8,128)S(1)}, bf16[96,256]{1,0:T(8,128)(2,1)S(...) custom-call(s32[1,2]{1,0:T(1,128)S(1)} %add_bitcast_fusion.scalars_ref, bf16[8,56,128]{2,1,0:T(8,128)(2,1)S(1)} %all_to_all.25.z_ref, ...), custom_call_target="tpu_custom_call" | custom-call | tf_op jit(solution)/shard_map/pallas_call | solution.py:222
  38.2 11.5 %all_to_all.26.incoming_ref = bf16[32,24,128]{2,1,0:T(8,128)(2,1)S(1)} all-to-all(bf16[32,24,128]{2,1,0:T(8,128)(2,1)S(1)} %get-tuple-element.16), channel_id=1, replica_groups=mesh['dom'=32,'blk'=8] {'dom'}, dimensions={0} | all-to-all | bytes 393216 | tf_op jit(solution)/shard_map/all_to_all | solution.py:167
  49.7 11.7 %all_to_all.27.z_ref = bf16[8,48,128]{2,1,0:T(8,128)(2,1)S(1)} all-to-all(bf16[8,48,128]{2,1,0:T(8,128)(2,1)S(1)} %shard_map.134), channel_id=1, replica_groups=mesh['dom'=32,'blk'=8] {'blk'}, dimensions={0} | all-to-all | bytes 196608 | tf_op jit(solution)/shard_map/all_to_all | solution.py:167
  61.4 0.0 copy-done.2
  61.4 0.0 copy-done.6
  61.4 0.0 copy-done.7
  61.4 2.5 %shard_map.135 = (f32[16,192]{1,0:T(8,128)S(1)}, f32[8,128]{1,0:T(8,128)S(1)}) custom-call(bf16[8,48,128]{2,1,0:T(8,128)(2,1)S(1)} %all_to_all.27.z_ref, bf16[96,256]{1,0:T(8,128)(2,1)S(1)} %get-tuple-element.18.main_ref, bf16[96,128]{1,0:T(8,128)(2,1)S(1)} %get-tuple-element.19.tail_ref, s32[96,64]{1,0:T(8,128)S(1)} %get-tuple-element.20.upper_ref, ...), custom_call_target="tpu_custom_call" | custom-call | tf_op jit(solution)/shard_map/pallas_call | solution.py:239
  63.9 10.1 %all_to_all.28.terms_ref = f32[8,1,128]{2,1,0:T(1,128)S(1)} all-to-all(f32[8,1,128]{2,1,0:T(1,128)S(1)} %bitcast.12), channel_id=1, replica_groups=mesh['dom'=32,'blk'=8] {'blk'}, dimensions={0} | all-to-all | bytes 8192 | tf_op jit(solution)/shard_map/all_to_all | solution.py:167
  74.0 0.6 shard_map.136
  (5 shorter events, 0.1 us)
Async XLA Ops:
  0.6 34.9 %copy-start.1 = (bf16[192,3072]{1,0:T(8,128)(2,1)S(1)}, bf16[192,3072]{1,0:T(8,128)(2,1)}, u32[]{:S(2)}) copy-start(bf16[192,3072]{1,0:T(8,128)(2,1)} %dinv.3) | copy-start | bytes 3538948
  0.6 34.9 %copy-start.5 = (f32[1024]{0:T(1024)S(1)}, f32[1024]{0:T(1024)}, u32[]{:S(2)}) copy-start(f32[1024]{0:T(1024)} %param.22) | copy-start | bytes 12292
  0.7 34.9 %copy-start.4 = (s32[16,6]{0,1:T(8,128)S(1)}, s32[16,6]{0,1:T(8,128)}, u32[]{:S(2)}) copy-start(s32[16,6]{0,1:T(8,128)} %param.16) | copy-start | bytes 1156
  0.7 34.9 %copy-start.3 = (bf16[16,192]{1,0:T(8,128)(2,1)S(1)}, bf16[16,192]{1,0:T(8,128)(2,1)}, u32[]{:S(2)}) copy-start(bf16[16,192]{1,0:T(8,128)(2,1)} %source_ref.1) | copy-start | bytes 18436
  2.3 15.3 %all-to-all-start = ((bf16[32,32,128]{2,1,0:T(8,128)(2,1)}), bf16[32,32,128]{2,1,0:T(8,128)(2,1)S(1)}, u32[]{:S(2)}, u32[]{:S(2)}) async-start(bf16[32,32,128]{2,1,0:T(8,128)(2,1)} %get-tuple-element.14), calls=%async_computation | async-start | bytes 524288 | tf_op jit(solution)/shard_map/all_to_all | solution.py:167
  17.6 17.9 %copy-start = (bf16[16,192,1152]{2,1,0:T(8,128)(2,1)S(1)}, bf16[16,192,1152]{2,1,0:T(8,128)(2,1)}, u32[]{:S(2)}) copy-start(bf16[16,192,1152]{2,1,0:T(8,128)(2,1)} %offd.3) | copy-start | bytes 21233668
  17.6 43.8 %copy-start.2 = (bf16[128,192]{0,1:T(8,128)(2,1)S(1)}, bf16[128,192]{0,1:T(8,128)(2,1)}, u32[]{:S(2)}) copy-start(bf16[128,192]{0,1:T(8,128)(2,1)} %param.21) | copy-start | bytes 147460
  17.6 43.8 %copy-start.6 = (s32[128]{0:T(128)S(1)}, s32[128]{0:T(128)}, u32[]{:S(2)}) copy-start(s32[128]{0:T(128)} %param.19) | copy-start | bytes 1540
  17.6 43.8 %copy-start.7 = (s32[128]{0:T(128)S(1)}, s32[128]{0:T(128)}, u32[]{:S(2)}) copy-start(s32[128]{0:T(128)} %param.20) | copy-start | bytes 1540

commit v5 on v4

--- a/solution.py
+++ b/solution.py
@@ -47,16 +47,40 @@
         message_ref[slot] = message
 
 
-def select_kernel(scalars_ref, incoming_ref, own_ref, *refs):
-    out_ref = refs[-1]
-    got = incoming_ref[jnp.max(scalars_ref[:, 0:1])].astype(F32)
+def first_select_kernel(scalars_ref, incoming_ref, own_ref, _, __, out_ref, face_ref):
+    got = select_kernel(scalars_ref, incoming_ref, own_ref, out_ref)
+    face_ref[...] = got[24:32]
+
+
+def select_kernel(scalars_ref, incoming_ref, own_ref, out_ref):
+    got = incoming_ref[jnp.max(scalars_ref[0:1, 0:1])].astype(F32)
     own = own_ref[...].astype(F32)
     rows = [own[0:16], got[0:16], own[16:24], got[16:24]]
-    if out_ref.shape[1] > 48:
-        rows.append(got[24:32])
     message = jnp.concatenate(rows, axis=0).astype(BF)
     for slot in range(N_BLK):
         out_ref[slot] = message
+    return got
+
+
+def second_select_kernel(scalars_ref, incoming_ref, own_ref, out_ref):
+    select_kernel(scalars_ref, incoming_ref, own_ref, out_ref)
+
+
+def prepare_kernel(
+    partner_ref, step_ref, columns_hbm, source_hbm, weights_hbm, forcing_ref, cols_ref, scalars_ref, columns, source, weights, square, sems
+):
+    scalars_ref[...] = jnp.full((8, 128), partner_ref[0], jnp.int32)
+    pairs = [(columns_hbm, columns), (source_hbm, source), (weights_hbm, weights)]
+    copies = [pltpu.make_async_copy(*pair, sems.at[i]) for i, pair in enumerate(pairs)]
+    for copy in copies:
+        copy.start()
+    for copy in copies:
+        copy.wait()
+    square[0:K, 0:BD] = columns[...]
+    cols_ref[...] = square[...].T[0:BD, :]
+    number = lax.broadcasted_iota(jnp.int32, (8, 128), 0) * 128 + lax.broadcasted_iota(jnp.int32, (8, 128), 1)
+    weight = jnp.sum(jnp.where(number == step_ref[0], weights[...], 0.0), keepdims=True)
+    forcing_ref[...] = source[...].astype(F32) * weight
 
 
 def gather_tables(face, columns, main_ref, tail_ref, upper_ref):
@@ -115,29 +139,20 @@
 
 
 def first_kernel(
-    scalars_ref,
+    face_ref,
     z_ref,
-    columns_ref,
-    source_ref,
-    weights_ref,
+    cols_ref,
+    forcing_ref,
     offd,
     dinv,
     out_ref,
     own_ref,
-    forcing_ref,
     main_ref,
     tail_ref,
     upper_ref,
-    square,
 ):
-    square[0:K, 0:BD] = columns_ref[...]
-    columns = square[...].T[0:BD, :]
-    face = z_ref[0].astype(F32)[48:49, 0:FB]
-    gather_tables(face, columns, main_ref, tail_ref, upper_ref)
-    number = lax.broadcasted_iota(jnp.int32, (8, 128), 0) * 128 + lax.broadcasted_iota(jnp.int32, (8, 128), 1)
-    weight = jnp.sum(jnp.where(number == scalars_ref[:, 1:2], weights_ref[...], 0.0), keepdims=True)
-    forcing = source_ref[...].astype(F32) * weight
-    forcing_ref[...] = forcing
+    gather_tables(face_ref[0:1, 0:FB], cols_ref[...], main_ref, tail_ref, upper_ref)
+    forcing = forcing_ref[...]
     total = sweep(z_ref, main_ref, tail_ref, upper_ref, forcing, offd, dinv)
     message = packed(total).astype(BF)
     own_ref[...] = message
@@ -192,6 +207,7 @@
     step_index,
 ):
     vmem = pl.BlockSpec(memory_space=pltpu.VMEM)
+    smem = pl.BlockSpec(memory_space=pltpu.SMEM)
     hbm = pl.BlockSpec(memory_space=pltpu.HBM)
 
     def shape(dims, dtype):
@@ -207,34 +223,49 @@
         scratch_shapes=[pltpu.VMEM((BD, BW), BF), pltpu.VMEM((1, FB), jnp.int32), pltpu.SemaphoreType.DMA((2,))],
         compiler_params=small,
     )(in_hbm(lam_init), in_hbm(face_list))
-    scalars = jnp.concatenate([partner, step_index]).reshape(1, 2)
-
-    def spread(incoming, own, rows, *unread):
-        return pl.pallas_call(
-            select_kernel,
-            out_shape=shape((N_BLK, rows, 128), BF),
-            in_specs=[vmem] * 3 + [hbm] * len(unread),
-            out_specs=vmem,
-            compiler_params=small,
-        )(scalars, incoming, own, *unread)
-
-    z1 = shift(spread(shift(message, "dom"), own, 56, in_hbm(offd), in_hbm(dinv)), "blk")
-    message, own, forcing, *tables = pl.pallas_call(
+    forcing, cols, scalars = pl.pallas_call(
+        prepare_kernel,
+        out_shape=(shape((BD, BW), F32), shape((BD, 128), jnp.int32), shape((8, 128), jnp.int32)),
+        in_specs=[smem] * 2 + [hbm] * 3,
+        out_specs=[vmem] * 3,
+        scratch_shapes=[
+            pltpu.VMEM((K, BD), jnp.int32),
+            pltpu.VMEM((BD, BW), BF),
+            pltpu.VMEM((8, 128), F32),
+            pltpu.VMEM((128, 128), jnp.int32),
+            pltpu.SemaphoreType.DMA((3,)),
+        ],
+        compiler_params=small,
+    )(partner, step_index, in_hbm(colidx.T), in_hbm(source), in_hbm(obj_weight.reshape(8, 128)))
+    z1, face = pl.pallas_call(
+        first_select_kernel,
+        out_shape=(shape((N_BLK, 48, 128), BF), shape((8, 128), F32)),
+        in_specs=[vmem] * 3 + [hbm] * 2,
+        out_specs=[vmem] * 2,
+        compiler_params=small,
+    )(scalars, shift(message, "dom"), own, in_hbm(offd), in_hbm(dinv))
+    z1 = shift(z1, "blk")
+    message, own, *tables = pl.pallas_call(
         first_kernel,
         out_shape=(
             shape((N_DOM, 24, 128), BF),
             shape((24, 128), BF),
-            shape((BD, BW), F32),
             shape((K * BD, N_BLK * 32), BF),
             shape((K * BD, N_BLK * 16), BF),
             shape((K * BD, 64), jnp.int32),
         ),
-        in_specs=[vmem] * 7,
-        out_specs=[vmem] * 6,
-        scratch_shapes=[pltpu.VMEM((128, 128), jnp.int32)],
+        in_specs=[vmem] * 6,
+        out_specs=[vmem] * 5,
         compiler_params=limit,
-    )(scalars, z1, colidx.T, source, obj_weight.reshape(8, 128), offd, dinv)
-    z2 = shift(spread(shift(message, "dom"), own, 48), "blk")
+    )(face, z1, cols, forcing, offd, dinv)
+    z2 = pl.pallas_call(
+        second_select_kernel,
+        out_shape=shape((N_BLK, 48, 128), BF),
+        in_specs=[vmem] * 3,
+        out_specs=vmem,
+        compiler_params=small,
+    )(scalars, shift(message, "dom"), own)
+    z2 = shift(z2, "blk")
     perf = perf_block.shape[0]
     adjoint, sums = pl.pallas_call(
         last_kernel,

time: 74.9 us -> 74.5 us (level)
  Pallas kernels: 7.41 us -> 8.22 us
  waiting for transfers between devices: 6.32 us -> 5.51 us
    pallas_call x2 -> x3, Pallas kernels: 0.09 us -> 0.96 us  [the longest x1 0.87 us: body(): pl.pallas_call(prepare_kernel, out_shape=(shape((BD, BW), F32), shape((BD...]
    all_to_all x1, waiting for transfers between devices: 6.32 us -> 5.51 us  [shift(): lax.all_to_all(message, axis, split_axis=0, concat_axis=0, tiled=True)]
  transfers between devices with their start and end apart: 1 -> 1, of which waited for: 1 -> 1; matrix products, arithmetic and copies ran while one was open for 0% -> 0% of each run, Pallas kernels for 0% -> 1%
where the time goes in v5:
time: 74.5 us; the launch traced here: 74.1 us
  blocking collectives  50.7 us (68%)
  Pallas kernels  8.22 us (11%)
  starting transfers between devices  7.63 us (10%)
  waiting for transfers between devices  5.51 us (7%)
  between operations  1.99 us (3%)
    all_to_all x4, blocking collectives, shift(): lax.all_to_all(message, axis, split_axis=0, concat_axis=0, tiled=True)  50.7 us
    all_to_all x1, starting transfers between devices, shift(): lax.all_to_all(message, axis, split_axis=0, concat_axis=0, tiled=True)  7.63 us
    all_to_all x1, waiting for transfers between devices, shift(): lax.all_to_all(message, axis, split_axis=0, concat_axis=0, tiled=True)  5.51 us
    pallas_call x1, Pallas kernels, body(): pl.pallas_call(first_kernel, out_shape=(shape((N_DOM, 24, 128), BF), shap...  2.55 us
    pallas_call x1, Pallas kernels, body(): pl.pallas_call(last_kernel, out_shape=(shape((BD, BW), F32), shape((N_BLK...  2.5 us
    pallas_call x1, Pallas kernels, body(): pl.pallas_call(entry_kernel, out_shape=(shape((N_DOM, 32, 128), BF), shap...  1.59 us
  transfers between devices with their start and end apart: 1, of which 1 were waited for; matrix products, arithmetic and copies ran while one was open for 0% of the time, Pallas kernels for 1%

profile of v5, /device:TPU:2, one launch (start us, length us, event | category | flops | bytes accessed | tf_op | source)
XLA Modules:
  0.0 74.1 jit_solution(1369300627493465568)
XLA Ops:
  0.6 0.0 copy-start.1
  0.6 1.6 %shard_map.132 = (bf16[32,32,128]{2,1,0:T(8,128)(2,1)}, bf16[32,128]{1,0:T(8,128)(2,1)S(1)}) custom-call(bf16[16,192]{1,0:T(8,128)(2,1)} %lam_hbm.1, s32[1,64]{1,0:T(1,128)} %face_hbm.1), custom_call_target="tpu_custom_call" | custom-call | tf_op jit(solution)/shard_map/pallas_call | solution.py:218
  2.2 7.6 %all-to-all-start = ((bf16[32,32,128]{2,1,0:T(8,128)(2,1)}), bf16[32,32,128]{2,1,0:T(8,128)(2,1)S(1)}, u32[]{:S(2)}, u32[]{:S(2)}) async-start(bf16[32,32,128]{2,1,0:T(8,128)(2,1)} %get-tuple-element.19), calls=%async_computation | async-start | bytes 524288 | tf_op jit(solution)/shard_map/all_to_all | solution.py:182
  11.2 0.9 %shard_map.131 = (f32[16,192]{1,0:T(8,128)S(1)}, s32[16,128]{1,0:T(8,128)S(1)}, s32[8,128]{1,0:T(8,128)S(1)}) custom-call(s32[1]{0:T(128)S(6)} %copy.14.partner_ref, s32[1]{0:T(128)S(6)} %copy.15.step_ref, s32[6,16]{1,0:T(8,128)} %bitcast.11, bf16[16,192]{1,0:T(8,128)(2,1)} %source_hbm.1, f32[8,128]{1,0:T(8,128)} %bitcast.12), custom_call_target="tpu_custom_call" | custom-call | tf_op jit(solution)/shard_map/pallas_call | solution.py:226
  12.1 5.5 %all-to-all-done.incoming_ref = bf16[32,32,128]{2,1,0:T(8,128)(2,1)S(1)} async-done(((bf16[32,32,128]{2,1,0:T(8,128)(2,1)}), bf16[32,32,128]{2,1,0:T(8,128)(2,1)S(1)}, u32[]{:S(2)}, u32[]{:S(2)}) %all-to-all-start) | async-done | bytes 262176 | tf_op jit(solution)/shard_map/all_to_all | solution.py:182
  17.6 0.0 copy-start
  17.6 0.0 copy-start.2
  17.6 0.0 copy-start.3
  17.6 0.0 copy-start.4
  17.6 17.5 %all_to_all.25.z_ref = bf16[8,48,128]{2,1,0:T(8,128)(2,1)S(1)} all-to-all(bf16[8,48,128]{2,1,0:T(8,128)(2,1)S(1)} %get-tuple-element.22), channel_id=1, replica_groups=mesh['dom'=32,'blk'=8] {'blk'}, dimensions={0} | all-to-all | bytes 196608 | tf_op jit(solution)/shard_map/all_to_all | solution.py:182
  35.1 0.0 copy-done.1
  35.1 0.0 copy-done
  35.1 2.5 %shard_map.134 = (bf16[32,24,128]{2,1,0:T(8,128)(2,1)S(1)}, bf16[24,128]{1,0:T(8,128)(2,1)S(1)}, bf16[96,256]{1,0:T(8,128)(2,1)S(1)}, bf16[96,128]{1,0:T(8,128)(2,1)S(1)}, s32[96,64]{1,0:T(8,128)S(1)}) custom-call(f32[8,128]{1,0:T(8,128)S(1)} %get-tuple-element.21.face_ref, bf16[8,48,128]{2,1,0:T(8,128)(2,1)S(1)} %all_to_all.25.z_ref, ...), custom_call_target="tpu_custom_call" | custom-call | tf_op jit(solution)/shard_map/pallas_call | solution.py:248
  37.7 11.5 %all_to_all.26.incoming_ref = bf16[32,24,128]{2,1,0:T(8,128)(2,1)S(1)} all-to-all(bf16[32,24,128]{2,1,0:T(8,128)(2,1)S(1)} %get-tuple-element.25), channel_id=1, replica_groups=mesh['dom'=32,'blk'=8] {'dom'}, dimensions={0} | all-to-all | bytes 393216 | tf_op jit(solution)/shard_map/all_to_all | solution.py:182
  49.3 11.7 %all_to_all.27.z_ref = bf16[8,48,128]{2,1,0:T(8,128)(2,1)S(1)} all-to-all(bf16[8,48,128]{2,1,0:T(8,128)(2,1)S(1)} %shard_map.135), channel_id=1, replica_groups=mesh['dom'=32,'blk'=8] {'blk'}, dimensions={0} | all-to-all | bytes 196608 | tf_op jit(solution)/shard_map/all_to_all | solution.py:182
  60.9 0.0 copy-done.2
  60.9 0.0 copy-done.3
  60.9 0.0 copy-done.4
  60.9 2.5 %shard_map.136 = (f32[16,192]{1,0:T(8,128)S(1)}, f32[8,128]{1,0:T(8,128)S(1)}) custom-call(bf16[8,48,128]{2,1,0:T(8,128)(2,1)S(1)} %all_to_all.27.z_ref, bf16[96,256]{1,0:T(8,128)(2,1)S(1)} %get-tuple-element.27.main_ref, bf16[96,128]{1,0:T(8,128)(2,1)S(1)} %get-tuple-element.28.tail_ref, s32[96,64]{1,0:T(8,128)S(1)} %get-tuple-element.29.upper_ref, ...), custom_call_target="tpu_custom_call" | custom-call | tf_op jit(solution)/shard_map/pallas_call | solution.py:270
  63.4 10.1 %all_to_all.28.terms_ref = f32[8,1,128]{2,1,0:T(1,128)S(1)} all-to-all(f32[8,1,128]{2,1,0:T(1,128)S(1)} %bitcast.8), channel_id=1, replica_groups=mesh['dom'=32,'blk'=8] {'blk'}, dimensions={0} | all-to-all | bytes 8192 | tf_op jit(solution)/shard_map/all_to_all | solution.py:182
  73.5 0.6 shard_map.137
  (2 shorter events, 0.1 us)
Async XLA Ops:
  0.6 34.5 %copy-start.1 = (bf16[192,3072]{1,0:T(8,128)(2,1)S(1)}, bf16[192,3072]{1,0:T(8,128)(2,1)}, u32[]{:S(2)}) copy-start(bf16[192,3072]{1,0:T(8,128)(2,1)} %dinv.3) | copy-start | bytes 3538948
  2.2 15.3 %all-to-all-start = ((bf16[32,32,128]{2,1,0:T(8,128)(2,1)}), bf16[32,32,128]{2,1,0:T(8,128)(2,1)S(1)}, u32[]{:S(2)}, u32[]{:S(2)}) async-start(bf16[32,32,128]{2,1,0:T(8,128)(2,1)} %get-tuple-element.19), calls=%async_computation | async-start | bytes 524288 | tf_op jit(solution)/shard_map/all_to_all | solution.py:182
  17.6 17.6 %copy-start = (bf16[16,192,1152]{2,1,0:T(8,128)(2,1)S(1)}, bf16[16,192,1152]{2,1,0:T(8,128)(2,1)}, u32[]{:S(2)}) copy-start(bf16[16,192,1152]{2,1,0:T(8,128)(2,1)} %offd.3) | copy-start | bytes 21233668
  17.6 43.4 %copy-start.2 = (bf16[128,192]{0,1:T(8,128)(2,1)S(1)}, bf16[128,192]{0,1:T(8,128)(2,1)}, u32[]{:S(2)}) copy-start(bf16[128,192]{0,1:T(8,128)(2,1)} %param.21) | copy-start | bytes 147460
  17.6 43.4 %copy-start.3 = (s32[128]{0:T(128)S(1)}, s32[128]{0:T(128)}, u32[]{:S(2)}) copy-start(s32[128]{0:T(128)} %param.19) | copy-start | bytes 1540
  17.6 43.4 %copy-start.4 = (s32[128]{0:T(128)S(1)}, s32[128]{0:T(128)}, u32[]{:S(2)}) copy-start(s32[128]{0:T(128)} %param.20) | copy-start | bytes 1540
